TPU v7x, 32 devices: a whole 2x2x4 slice. The times are simulated.
32 devices in a mesh: group: 2 (over y), col: 4 (over z), sec: 2 (over x), lev: 2 (over core).
Axes of the slice: x: 2, y: 2, z: 4, core: 2. Of those that a mesh axis runs over, the one named last changes fastest.
Arguments:
- thermal_departure: bfloat16 [60, 512, 512], P('lev', ('group', 'col'), 'sec'), parts along dimension 1, may hold values from -6 to 6
- seed_sensitivity: float32 [60, 512, 512], P('lev', ('group', 'col'), 'sec'), parts along dimension 1, may hold values from -6 to 6
- zonal_flow_ratio: float32 [60, 512, 512], P('lev', ('group', 'col'), 'sec'), parts along dimension 1, may hold values from 0.3 to 0.6
- meridional_flow_ratio: float32 [60, 512, 512], P('lev', ('group', 'col'), 'sec'), parts along dimension 1, may hold values from 0.05 to 0.2
- updraft_flow_ratio: float32 [60, 512, 512], P('lev', ('group', 'col'), 'sec'), parts along dimension 1, may hold values from 0.05 to 0.2
- entry_layer_matrix: float32 [60, 256], replicated, may hold values from -0.75 to 0.75
- final_layer_matrix: float32 [256, 60], replicated, may hold values from -0.375 to 0.375
- mean_estimate_entry_matrix: float32 [60, 256], P(None, ('col', 'sec', 'lev')), may hold values from -6 to 6
- squared_estimate_entry_matrix: float32 [60, 256], P(None, ('col', 'sec', 'lev')), may hold values from 0.1 to 2
- mean_estimate_final_matrix: float32 [256, 60], P(('col', 'sec', 'lev')), may hold values from -6 to 6
- squared_estimate_final_matrix: float32 [256, 60], P(('col', 'sec', 'lev')), may hold values from 0.1 to 2
Outputs:
- input_cotangent: float32 [60, 512, 512], P('lev', ('group', 'col'), 'sec'), parts along dimension 1
- new_w_in: float32 [120, 256], P('group'), parts along dimension 0
- new_w_out: float32 [512, 60], P('group'), parts along dimension 0
- new_first_in: float32 [120, 256], P('group', ('col', 'sec', 'lev')), parts along dimension 0
- new_second_in: float32 [120, 256], P('group', ('col', 'sec', 'lev')), parts along dimension 0
- new_first_out: float32 [512, 60], P(('group', 'col', 'sec', 'lev')), parts along dimension 0
- new_second_out: float32 [512, 60], P(('group', 'col', 'sec', 'lev')), parts along dimension 0
There are 2 independent parts, one for each index of `group`. A program takes and returns all parts, laid end to end along the dimension named above; an argument that names none is the same for every part. Nothing has to cross between parts.
All inputs are finite; a program needn't handle non-finite values.
Results may differ from a plain program's by a relative error of at most 0.0003.
The roundings to bfloat16 on the way count: a program that leaves them out, or rounds other values in their place, can miss the bound.
Values may be sent and summed in bfloat16 or wider, within the bound.
A program may use at most 128 MiB of HBM per device.

v0:
```python
import math

import jax
import jax.numpy as jnp
from jax import lax
from jax.sharding import PartitionSpec as P

STEPS = 4


bias_first = 1.0 - 0.9**10
bias_second = 1.0 - 0.999**10


def passed_along(value, axis, steps):
    count = lax.axis_size(axis)
    pairs = [(source, (source + steps) % count) for source in range(count)]
    return lax.ppermute(value, axis, pairs)


def from_behind(value, axis, steps):
    count = lax.axis_size(axis)
    first, last = (max(0, -steps), min(count, count - steps))
    return lax.ppermute(value, axis, [(source, source + steps) for source in range(first, last)])


def adam_update(weight, grad, first, second):
    new_first = 0.9 * first + 0.1 * grad
    new_second = 0.999 * second + 0.001 * grad * grad
    step_size = new_first / bias_first / (jnp.sqrt(new_second / bias_second) + 1e-08)
    return (weight - 0.01 * step_size, new_first, new_second)


def adjoint_step(costate, zonal_flow_ratio, meridional_flow_ratio, updraft_flow_ratio):
    edge_x = passed_along(costate[:, 0:1, :], "col", -1)
    edge_y = from_behind(costate[:, :, 0:1], "sec", -1)
    edge_z = from_behind(costate[0:1], "lev", -1)
    next_x = jnp.concatenate([costate[:, 1:, :], edge_x], axis=1)
    next_y = jnp.concatenate([costate[:, :, 1:], edge_y], axis=2)
    next_z = jnp.concatenate([costate[1:], edge_z], axis=0)
    return (
        costate
        + zonal_flow_ratio * (next_x - costate)
        + meridional_flow_ratio * (next_y - costate)
        + updraft_flow_ratio * (next_z - costate)
    )


def transport(seed_sensitivity, zonal_flow_ratio, meridional_flow_ratio, updraft_flow_ratio):
    costate = seed_sensitivity
    for step in range(STEPS):
        costate = adjoint_step(costate, zonal_flow_ratio, meridional_flow_ratio, updraft_flow_ratio)
    return costate


def shards(
    thermal_departure,
    seed_sensitivity,
    zonal_flow_ratio,
    meridional_flow_ratio,
    updraft_flow_ratio,
    entry_layer_matrix,
    final_layer_matrix,
    mean_estimate_entry_matrix,
    squared_estimate_entry_matrix,
    mean_estimate_final_matrix,
    squared_estimate_final_matrix,
):
    levels_all = entry_layer_matrix.shape[0]
    w_in_bf = entry_layer_matrix.astype(jnp.bfloat16)
    w_out_bf = final_layer_matrix.astype(jnp.bfloat16)
    total_cols = (
        seed_sensitivity.shape[1]
        * seed_sensitivity.shape[2]
        * lax.axis_size("col")
        * lax.axis_size("sec")
    )
    factor = 1.0 / math.sqrt(total_cols)
    costate = transport(
        seed_sensitivity, zonal_flow_ratio, meridional_flow_ratio, updraft_flow_ratio
    )
    costate_bf = costate.astype(jnp.bfloat16)
    profiles, back_cols = (
        lax.all_to_all(thermal_departure, "lev", split_axis=1, concat_axis=0, tiled=True),
        lax.all_to_all(costate_bf, "lev", split_axis=1, concat_axis=0, tiled=True),
    )
    flat = profiles.reshape(levels_all, -1)
    pre = lax.dot_general(
        w_in_bf, flat, (((0,), (0,)), ((), ())), preferred_element_type=jnp.float32
    )
    act = jnp.tanh(pre)
    col_shape = back_cols.shape
    back = back_cols.reshape(levels_all, -1)
    act_bf = act.astype(jnp.bfloat16)
    part_out = lax.dot_general(
        act_bf, back, (((1,), (1,)), ((), ())), preferred_element_type=jnp.float32
    )
    d_act = jnp.dot(w_out_bf, back, preferred_element_type=jnp.float32)
    d_pre = (d_act * (1.0 - act * act)).astype(jnp.bfloat16)
    part_in = lax.dot_general(
        flat, d_pre, (((1,), (1,)), ((), ())), preferred_element_type=jnp.float32
    )
    d_input = jnp.dot(w_in_bf, d_pre, preferred_element_type=jnp.float32).astype(jnp.bfloat16)
    d_levels = lax.all_to_all(
        d_input.reshape(col_shape), "lev", split_axis=0, concat_axis=1, tiled=True
    )
    input_cotangent = costate + d_levels.astype(jnp.float32)
    part_in = part_in * factor
    part_out = part_out * factor
    share = mean_estimate_entry_matrix.shape[1]
    leading_position = lax.axis_index(("col", "sec", "lev")) * share
    grad_in, grad_out = (
        lax.psum_scatter(part_in, ("col", "sec", "lev"), scatter_dimension=1, tiled=True),
        lax.psum_scatter(part_out, ("col", "sec", "lev"), scatter_dimension=0, tiled=True),
    )
    own_in = lax.dynamic_slice_in_dim(entry_layer_matrix, leading_position, share, 1)
    own_out = lax.dynamic_slice_in_dim(final_layer_matrix, leading_position, share, 0)
    piece_in, new_first_in, new_second_in = adam_update(
        own_in, grad_in, mean_estimate_entry_matrix, squared_estimate_entry_matrix
    )
    piece_out, new_first_out, new_second_out = adam_update(
        own_out, grad_out, mean_estimate_final_matrix, squared_estimate_final_matrix
    )
    new_w_in, new_w_out = (
        lax.all_gather(piece_in, ("col", "sec", "lev"), axis=1, tiled=True),
        lax.all_gather(piece_out, ("col", "sec", "lev"), axis=0, tiled=True),
    )
    return (
        input_cotangent,
        new_w_in,
        new_w_out,
        new_first_in,
        new_second_in,
        new_first_out,
        new_second_out,
    )


def solution(mesh):
    in_specs = (
        P("lev", ("group", "col"), "sec"),
        P("lev", ("group", "col"), "sec"),
        P("lev", ("group", "col"), "sec"),
        P("lev", ("group", "col"), "sec"),
        P("lev", ("group", "col"), "sec"),
        P(),
        P(),
        P(None, ("col", "sec", "lev")),
        P(None, ("col", "sec", "lev")),
        P(("col", "sec", "lev"), None),
        P(("col", "sec", "lev"), None),
    )
    out_specs = (
        P("lev", ("group", "col"), "sec"),
        P("group", None),
        P("group", None),
        P("group", ("col", "sec", "lev")),
        P("group", ("col", "sec", "lev")),
        P(("group", "col", "sec", "lev"), None),
        P(("group", "col", "sec", "lev"), None),
    )
    return jax.shard_map(shards, mesh=mesh, in_specs=in_specs, out_specs=out_specs, check_vma=False)
```

profile of v0, /device:TPU:0, one launch (start us, length us, event | category | flops | bytes accessed | tf_op | source)
XLA Modules:
  0.0 268.3 jit_solution(14146019828793476657)
XLA Ops:
  10.4 5.1 %collective-permute-start = (f32[30,1,256]{2,1,0:T(1,128)S(1)}, f32[30,1,256]{2,1,0:T(1,128)S(1)}, u32[]{:S(2)}, u32[]{:S(2)}) collective-permute-start(f32[30,1,256]{2,1,0:T(1,128)S(1)} %slice.73), channel_id=1, source_target_pairs={{0,12},{4,0},{8,4},{12,8},{1,13},{5,1},{9,5},{13,9},{2,14},{6,2},{... | collective-permute-start | bytes 92168 | tf_op jit(solution)/shard_map/ppermute | solution.py:18
  17.3 2.7 %copy.147 = bf16[30,64,256]{2,0,1:T(8,128)(2,1)} copy(bf16[30,64,256]{2,1,0:T(8,128)(2,1)} %param.11) | data formatting | bytes 1966080 | tf_op args[0]
  20.0 3.6 %all-to-all-start.1 = ((bf16[30,64,256]{2,0,1:T(8,128)(2,1)}), bf16[30,64,256]{2,0,1:T(8,128)(2,1)S(1)}, u32[]{:S(2)}, u32[]{:S(2)}) async-start(bf16[30,64,256]{2,0,1:T(8,128)(2,1)} %copy.147), calls=%async_computation.1 | async-start | bytes 2097152 | tf_op jit(solution)/shard_map/all_to_all | solution.py:84
  25.0 1.9 slice.74
  31.0 6.9 %fusion.7 = f32[30,64,256]{2,1,0:T(8,128)S(1)} fusion(f32[30,64,256]{2,1,0:T(8,128)} %param.12, f32[30,64,256]{2,1,0:T(8,128)} %param.13, f32[30,1,256]{2,1,0:T(1,128)S(1)} %collective-permute-done, f32[30,63,256]{2,1,0:T(8,128)} %slice.72, f32[30,64,256]{2,1,0:T(8,128)} %param.14, f32[30,64,1]{2,1,0:T(8,128)} %copy.138, f32[30,64,255]{2,1,0:T(8,128)} %slice.74, ...), kind=kLoop, calls=%fused_computation.11 | loop fusion | flops 5898240 | bytes 15728640 | tf_op jit(solution)/shard_map/add | solution.py:42
  40.7 1.6 copy.139
  43.6 4.7 %convolution_tanh_fusion = f32[256,8192]{0,1:T(8,128)} fusion(bf16[60,8192]{1,0:T(8,128)(2,1)S(1)} %bitcast.47, f32[60,256]{1,0:T(8,128)S(1)} %copy-done.3), kind=kOutput, calls=%fused_computation | convolution fusion | flops 251673600 | bytes 9433088 | tf_op jit(solution)/shard_map/dot_general | solution.py:88
  49.7 1.9 slice.98
  54.6 6.3 %fusion.13 = f32[30,64,256]{2,1,0:T(8,128)S(1)} fusion(f32[30,64,256]{2,1,0:T(8,128)S(1)} %fusion.7, f32[30,64,256]{2,1,0:T(8,128)} %param.13, f32[30,1,256]{2,1,0:T(1,128)S(1)} %collective-permute-done.3, f32[30,63,256]{2,1,0:T(8,128)} %slice.96, f32[30,64,256]{2,1,0:T(8,128)} %param.14, f32[30,64,1]{2,1,0:T(8,128)} %copy.140, f32[30,64,255]{2,1,0:T(8,128)} %slice.98, ...), kind=kLoop, calls=%fused_computation.20 | loop fusion | flops 5898240 | bytes 15728640 | tf_op jit(solution)/shard_map/add | solution.py:42
  64.5 1.6 collective-permute-start.7
  66.2 3.0 %slice.106 = f32[29,64,256]{2,1,0:T(8,128)} slice(f32[30,64,256]{2,1,0:T(8,128)} %copy-done), slice={[1:30], [0:64], [0:256]} | slice | bytes 3801088 | tf_op jit(solution)/shard_map/slice | solution.py:40
  69.2 1.9 slice.104
  73.9 6.9 %fusion.19 = f32[30,64,256]{2,1,0:T(8,128)S(1)} fusion(f32[30,64,256]{2,1,0:T(8,128)} %copy-done, f32[30,64,256]{2,1,0:T(8,128)} %param.13, f32[30,1,256]{2,1,0:T(1,128)S(1)} %collective-permute-done.6, f32[30,63,256]{2,1,0:T(8,128)} %slice.102, f32[30,64,256]{2,1,0:T(8,128)} %param.14, f32[30,64,1]{2,1,0:T(8,128)} %copy.142, f32[30,64,255]{2,1,0:T(8,128)} %slice.104, ...), kind=kLoop, calls=%fused_computation.29 | loop fusion | flops 5898240 | bytes 15728640 | tf_op jit(solution)/shard_map/add | solution.py:42
  87.8 1.8 slice.110
  92.5 7.0 %fusion.41 = (bf16[30,64,256]{2,1,0:T(8,128)(2,1)S(1)}, f32[30,64,256]{2,1,0:T(8,128)}) fusion(f32[30,64,256]{2,1,0:T(8,128)} %param.15, f32[30,64,256]{2,1,0:T(8,128)S(1)} %fusion.19, f32[1,64,256]{2,1,0:T(8,128)S(1)} %collective-permute-done.11, f32[29,64,256]{2,1,0:T(8,128)} %slice.112, f32[30,64,256]{2,1,0:T(8,128)} %param.14, f32[30,64,1]{2,1,0:T(8,128)} %copy.144, ...), kind=kLoop, calls=%fused_computation.62 | loop fusion | flops 6389760 | bytes 16711680 | tf_op jit(solution)/shard_map/convert_element_type | solution.py:82
  100.1 5.2 %all_to_all.39 = bf16[30,64,256]{2,0,1:T(8,128)(2,1)S(1)} all-to-all(bf16[30,64,256]{2,0,1:T(8,128)(2,1)S(1)} %copy.145), channel_id=1, replica_groups=mesh['group'=2,'col'=4,'sec'=2,'lev'=2] {'lev'}, dimensions={1} | all-to-all | bytes 1966080 | tf_op jit(solution)/shard_map/all_to_all | solution.py:85
  106.6 4.4 %fusion.28 = f32[256,60]{0,1:T(8,128)S(1)} fusion(bf16[60,8192]{1,0:T(8,128)(2,1)S(1)} %bitcast.49, f32[256,8192]{0,1:T(8,128)} %convolution_tanh_fusion), kind=kOutput, calls=%fused_computation.45 | convolution fusion | flops 253770752 | bytes 9433088 | tf_op jit(solution)/shard_map/dot_general | solution.py:95
  116.2 3.6 %all-to-all-start.2 = ((bf16[60,32,256]{2,1,0:T(8,128)(2,1)}), bf16[60,32,256]{2,1,0:T(8,128)(2,1)S(1)}, u32[]{:S(2)}, u32[]{:S(2)}) async-start(bf16[60,32,256]{2,1,0:T(8,128)(2,1)} %slice.114), calls=%async_computation.2 | async-start | bytes 1966080 | tf_op jit(solution)/shard_map/all_to_all | solution.py:104
  124.1 1.7 copy.150
  125.8 3.2 %bitcast_add_fusion = f32[30,64,256]{2,1,0:T(8,128)} fusion(f32[30,64,256]{2,1,0:T(8,128)} %get-tuple-element.56, f32[30,2,32,256]{3,2,1,0:T(8,128)S(1)} %copy.150), kind=kLoop, calls=%fused_computation.44 | loop fusion | flops 491520 | bytes 5898240 | tf_op jit(solution)/shard_map/add | solution.py:107
  129.0 53.1 %reduce-scatter.9.cloned.1.call-done = f32[16,60]{1,0:T(8,128)} async-done(((f32[256,60]{1,0:T(8,128)}), f32[16,60]{1,0:T(8,128)}) %reduce-scatter.9.cloned.1.call-update) | async-done | bytes 3856 | tf_op jit(solution)/shard_map/reduce_scatter | solution.py:114
  183.4 19.7 %all_gather.7 = f32[256,60]{1,0:T(8,128)S(1)} all-gather(f32[16,60]{1,0:T(8,128)S(1)} %get-tuple-element.49), channel_id=1, replica_groups=mesh['group'=2,'col'=4,'sec'=2,'lev'=2] {'col','sec','lev'}, dimensions={0}, use_global_device_ids=true | all-gather | bytes 65280 | tf_op jit(solution)/shard_map/all_gather | solution.py:126
  203.8 35.8 %reduce-scatter.7.cloned.1.call-done = f32[16,60]{1,0:T(8,128)} async-done(((f32[256,60]{1,0:T(8,128)}), f32[16,60]{1,0:T(8,128)}) %reduce-scatter.7.cloned.1.call-update) | async-done | bytes 3856
  241.0 19.7 %all_gather.6 = f32[60,256]{0,1:T(8,128)S(1)} all-gather(f32[60,16]{0,1:T(8,128)S(1)} %get-tuple-element.52), channel_id=1, replica_groups=mesh['group'=2,'col'=4,'sec'=2,'lev'=2] {'col','sec','lev'}, dimensions={1}, use_global_device_ids=true | all-gather | bytes 65280 | tf_op jit(solution)/shard_map/all_gather | solution.py:125
  (101 shorter events, 50.6 us)
Async XLA Ops:
  7.2 8.3 %slice-start.2 = ((f32[30,64,256]{2,1,0:T(8,128)}), f32[30,64,1]{2,1,0:T(8,128)S(1)}, s32[]{:S(2)}) async-start(f32[30,64,256]{2,1,0:T(8,128)} %param.12), calls=%async_computation.9 | async-start | bytes 1966080 | tf_op jit(solution)/shard_map/slice | solution.py:36
  8.1 22.9 %collective-permute-start.2 = (f32[1,64,256]{2,1,0:T(8,128)S(1)}, f32[1,64,256]{2,1,0:T(8,128)S(1)}, u32[]{:S(2)}, u32[]{:S(2)}) collective-permute-start(f32[1,64,256]{2,1,0:T(8,128)S(1)} %slice.77), channel_id=1, source_target_pairs={{1,0},{3,2},{5,4},{7,6},{9,8},{11,10},{13,12},{15,14},{17,16},{19,... | collective-permute-start | bytes 196616 | tf_op jit(solution)/shard_map/ppermute | solution.py:24
  10.4 20.7 %collective-permute-start = (f32[30,1,256]{2,1,0:T(1,128)S(1)}, f32[30,1,256]{2,1,0:T(1,128)S(1)}, u32[]{:S(2)}, u32[]{:S(2)}) collective-permute-start(f32[30,1,256]{2,1,0:T(1,128)S(1)} %slice.73), channel_id=1, source_target_pairs={{0,12},{4,0},{8,4},{12,8},{1,13},{5,1},{9,5},{13,9},{2,14},{6,2},{... | collective-permute-start | bytes 92168 | tf_op jit(solution)/shard_map/ppermute | solution.py:18
  15.8 7.8 %copy-start.2 = (f32[30,64,256]{2,1,0:T(8,128)S(1)}, f32[30,64,256]{2,1,0:T(8,128)}, u32[]{:S(2)}) copy-start(f32[30,64,256]{2,1,0:T(8,128)} %param.12) | copy-start | bytes 5898244
  15.8 13.9 %collective-permute-start.1 = (f32[30,64,1]{1,0,2:T(8,128)S(1)}, f32[30,64,1]{1,0,2:T(8,128)S(1)}, u32[]{:S(2)}, u32[]{:S(2)}) collective-permute-start(f32[30,64,1]{1,0,2:T(8,128)S(1)} %copy.168), channel_id=1, source_target_pairs={{2,0},{3,1},{6,4},{7,5},{10,8},{11,9},{14,12},{15,13},{18,16},{19,... | collective-permute-start | bytes 23048 | tf_op jit(solution)/shard_map/ppermute | solution.py:24
  20.0 8.4 %all-to-all-start.1 = ((bf16[30,64,256]{2,0,1:T(8,128)(2,1)}), bf16[30,64,256]{2,0,1:T(8,128)(2,1)S(1)}, u32[]{:S(2)}, u32[]{:S(2)}) async-start(bf16[30,64,256]{2,0,1:T(8,128)(2,1)} %copy.147), calls=%async_computation.1 | async-start | bytes 2097152 | tf_op jit(solution)/shard_map/all_to_all | solution.py:84
  37.9 5.7 %copy-start.3 = (f32[60,256]{1,0:T(8,128)S(1)}, f32[60,256]{1,0:T(8,128)}, u32[]{:S(2)}) copy-start(f32[60,256]{1,0:T(8,128)} %param.16) | copy-start | bytes 184324
  39.0 15.6 %collective-permute-start.3 = (f32[30,1,256]{2,1,0:T(1,128)S(1)}, f32[30,1,256]{2,1,0:T(1,128)S(1)}, u32[]{:S(2)}, u32[]{:S(2)}) collective-permute-start(f32[30,1,256]{2,1,0:T(1,128)S(1)} %slice.97), channel_id=1, source_target_pairs={{0,12},{4,0},{8,4},{12,8},{1,13},{5,1},{9,5},{13,9},{2,14},{6,2},{... | collective-permute-start | bytes 92168 | tf_op jit(solution)/shard_map/ppermute | solution.py:18
  39.5 15.2 %collective-permute-start.5 = (f32[1,64,256]{2,1,0:T(8,128)S(1)}, f32[1,64,256]{2,1,0:T(8,128)S(1)}, u32[]{:S(2)}, u32[]{:S(2)}) collective-permute-start(f32[1,64,256]{2,1,0:T(8,128)S(1)} %slice.101), channel_id=1, source_target_pairs={{1,0},{3,2},{5,4},{7,6},{9,8},{11,10},{13,12},{15,14},{17,16},{19,... | collective-permute-start | bytes 196616 | tf_op jit(solution)/shard_map/ppermute | solution.py:24
  42.3 10.9 %collective-permute-start.4 = (f32[30,64,1]{1,0,2:T(8,128)S(1)}, f32[30,64,1]{1,0,2:T(8,128)S(1)}, u32[]{:S(2)}, u32[]{:S(2)}) collective-permute-start(f32[30,64,1]{1,0,2:T(8,128)S(1)} %copy.139), channel_id=1, source_target_pairs={{2,0},{3,1},{6,4},{7,5},{10,8},{11,9},{14,12},{15,13},{18,16},{19,... | collective-permute-start | bytes 23048 | tf_op jit(solution)/shard_map/ppermute | solution.py:24
  62.3 11.6 %collective-permute-start.6 = (f32[30,1,256]{2,1,0:T(1,128)S(1)}, f32[30,1,256]{2,1,0:T(1,128)S(1)}, u32[]{:S(2)}, u32[]{:S(2)}) collective-permute-start(f32[30,1,256]{2,1,0:T(1,128)S(1)} %slice.103), channel_id=1, source_target_pairs={{0,12},{4,0},{8,4},{12,8},{1,13},{5,1},{9,5},{13,9},{2,14},{6,2},{... | collective-permute-start | bytes 92168 | tf_op jit(solution)/shard_map/ppermute | solution.py:18
  62.8 11.1 %collective-permute-start.8 = (f32[1,64,256]{2,1,0:T(8,128)S(1)}, f32[1,64,256]{2,1,0:T(8,128)S(1)}, u32[]{:S(2)}, u32[]{:S(2)}) collective-permute-start(f32[1,64,256]{2,1,0:T(8,128)S(1)} %slice.107), channel_id=1, source_target_pairs={{1,0},{3,2},{5,4},{7,6},{9,8},{11,10},{13,12},{15,14},{17,16},{19,... | collective-permute-start | bytes 196616 | tf_op jit(solution)/shard_map/ppermute | solution.py:24
  64.5 8.1 %collective-permute-start.7 = (f32[30,64,1]{1,0,2:T(8,128)S(1)}, f32[30,64,1]{1,0,2:T(8,128)S(1)}, u32[]{:S(2)}, u32[]{:S(2)}) collective-permute-start(f32[30,64,1]{1,0,2:T(8,128)S(1)} %copy.141), channel_id=1, source_target_pairs={{2,0},{3,1},{6,4},{7,5},{10,8},{11,9},{14,12},{15,13},{18,16},{19,... | collective-permute-start | bytes 23048 | tf_op jit(solution)/shard_map/ppermute | solution.py:24
  81.9 10.6 %collective-permute-start.9 = (f32[30,1,256]{2,1,0:T(1,128)S(1)}, f32[30,1,256]{2,1,0:T(1,128)S(1)}, u32[]{:S(2)}, u32[]{:S(2)}) collective-permute-start(f32[30,1,256]{2,1,0:T(1,128)S(1)} %slice.109), channel_id=1, source_target_pairs={{0,12},{4,0},{8,4},{12,8},{1,13},{5,1},{9,5},{13,9},{2,14},{6,2},{... | collective-permute-start | bytes 92168 | tf_op jit(solution)/shard_map/ppermute | solution.py:18
  81.9 10.6 %collective-permute-start.11 = (f32[1,64,256]{2,1,0:T(8,128)S(1)}, f32[1,64,256]{2,1,0:T(8,128)S(1)}, u32[]{:S(2)}, u32[]{:S(2)}) collective-permute-start(f32[1,64,256]{2,1,0:T(8,128)S(1)} %slice.113), channel_id=1, source_target_pairs={{1,0},{3,2},{5,4},{7,6},{9,8},{11,10},{13,12},{15,14},{17,16},{19,... | collective-permute-start | bytes 196616 | tf_op jit(solution)/shard_map/ppermute | solution.py:24
  84.8 6.4 %collective-permute-start.10 = (f32[30,64,1]{1,0,2:T(8,128)S(1)}, f32[30,64,1]{1,0,2:T(8,128)S(1)}, u32[]{:S(2)}, u32[]{:S(2)}) collective-permute-start(f32[30,64,1]{1,0,2:T(8,128)S(1)} %copy.143), channel_id=1, source_target_pairs={{2,0},{3,1},{6,4},{7,5},{10,8},{11,9},{14,12},{15,13},{18,16},{19,... | collective-permute-start | bytes 23048 | tf_op jit(solution)/shard_map/ppermute | solution.py:24
  105.3 5.7 %slice-start = ((s8[8388608]{0:T(1024)(128)(4,1)}), s8[4194304]{0:T(1024)(128)(4,1)S(1)}, s32[]{:S(2)}) async-start(s8[8388608]{0:T(1024)(128)(4,1)} %bitcast.45), calls=%async_computation.7 | async-start | bytes 8388608
  116.2 5.6 %all-to-all-start.2 = ((bf16[60,32,256]{2,1,0:T(8,128)(2,1)}), bf16[60,32,256]{2,1,0:T(8,128)(2,1)S(1)}, u32[]{:S(2)}, u32[]{:S(2)}) async-start(bf16[60,32,256]{2,1,0:T(8,128)(2,1)} %slice.114), calls=%async_computation.2 | async-start | bytes 1966080 | tf_op jit(solution)/shard_map/all_to_all | solution.py:104
  119.8 62.3 %reduce-scatter.9.cloned.1.call-start = ((), (), s32[]{:S(2)}) async-start(), calls=%async_computation.6 | async-start | bytes 139264 | tf_op jit(solution)/shard_map/reduce_scatter | solution.py:114
  120.6 119.1 %reduce-scatter.7.cloned.1.call-start = ((), (), s32[]{:S(2)}) async-start(), calls=%async_computation.5 | async-start | bytes 139264
  125.8 56.3 %copy-start.5 = (f32[16,60]{1,0:T(8,128)S(1)}, f32[16,60]{1,0:T(8,128)}, u32[]{:S(2)}) copy-start(f32[16,60]{1,0:T(8,128)} %param.20) | copy-start | bytes 11524
  125.8 56.3 %copy-start.6 = (f32[16,60]{1,0:T(8,128)S(1)}, f32[16,60]{1,0:T(8,128)}, u32[]{:S(2)}) copy-start(f32[16,60]{1,0:T(8,128)} %param.21) | copy-start | bytes 11524
  125.8 113.9 %copy-start.7 = (f32[60,16]{0,1:T(8,128)S(1)}, f32[60,16]{0,1:T(8,128)}, u32[]{:S(2)}) copy-start(f32[60,16]{0,1:T(8,128)} %param.18) | copy-start | bytes 11524
  125.8 113.8 %copy-start.8 = (f32[60,16]{0,1:T(8,128)S(1)}, f32[60,16]{0,1:T(8,128)}, u32[]{:S(2)}) copy-start(f32[60,16]{0,1:T(8,128)} %param.19) | copy-start | bytes 11524
  (4 other events, 16.0 us)
Sparse Core Ops, SparseCore 0:
  124.1 57.9 reduce-scatter.8
  185.5 54.0 reduce-scatter.6
where the time goes:
time: 269 us; the launch traced here: 268 us
  waiting for transfers between devices  90.2 us (34%)
  local copies, waits for them, and re-layouts  48 us (18%)
  blocking collectives  44.7 us (17%)
  other arithmetic  34.4 us (13%)
  starting transfers between devices  24.1 us (9%)
  between operations  14.4 us (5%)
  matrix products  12.6 us (5%)
    reduce_scatter x1, waiting for transfers between devices, shards(): lax.psum_scatter(part_out, ('col', 'sec', 'lev'), scatter_dimension=0, ti...  53.1 us
    unnamed x3, waiting for transfers between devices  35.9 us
    add x3, other arithmetic, adjoint_step(): costate + zonal_flow_ratio * (next_x - costate)  20.1 us
    all_gather x1, blocking collectives, shards(): lax.all_gather(piece_in, ('col', 'sec', 'lev'), axis=1, tiled=True)  19.7 us
    all_gather x1, blocking collectives, shards(): lax.all_gather(piece_out, ('col', 'sec', 'lev'), axis=0, tiled=True)  19.7 us
    ppermute x8, starting transfers between devices, from_behind(): lax.ppermute(value, axis, [(source, source + steps) for source in range(f...  10.8 us
    unnamed x35, local copies, waits for them, and re-layouts  9.51 us
    slice x4, local copies, waits for them, and re-layouts, adjoint_step(): next_y = jnp.concatenate([costate[:, :, 1:], edge_y], axis=2)  7.47 us
  transfers between devices with their start and end apart: 16, of which 3 were waited for; matrix products, arithmetic and copies ran while one was open for 19% of the time, Pallas kernels for 0%

commit v1 on v0

--- a/solution.py
+++ b/solution.py
@@ -1,8 +1,11 @@
+import functools
 import math
 
 import jax
 import jax.numpy as jnp
 from jax import lax
+from jax.experimental import pallas as pl
+from jax.experimental.pallas import tpu as pltpu
 from jax.sharding import PartitionSpec as P
 
 STEPS = 4
@@ -51,6 +54,131 @@
     for step in range(STEPS):
         costate = adjoint_step(costate, zonal_flow_ratio, meridional_flow_ratio, updraft_flow_ratio)
     return costate
+
+
+MESH = pl.DeviceIdType.MESH
+REDUCED = ("col", "sec", "lev")
+
+
+def slot_size(levels):
+    return -(-levels // 8) * 8
+
+
+def slots(value, parts):
+    levels = value.shape[1] // parts
+    value = value.reshape(value.shape[0], parts, levels)
+    value = jnp.pad(value, ((0, 0), (0, 0), (0, slot_size(levels) - levels)))
+    return value.reshape(value.shape[0], -1)
+
+
+def unslots(value, parts, levels_all):
+    slot = value.shape[1] // parts
+    value = value.reshape(value.shape[0], parts, slot)[:, :, : levels_all // parts]
+    return value.reshape(value.shape[0], levels_all)
+
+
+def peer_at(position, sizes):
+    _, secs, levs = sizes
+    return {
+        "col": lax.div(position, secs * levs),
+        "sec": lax.rem(lax.div(position, levs), secs),
+        "lev": lax.rem(position, levs),
+    }
+
+
+def own_position(sizes):
+    _, secs, levs = sizes
+    return (lax.axis_index("col") * secs + lax.axis_index("sec")) * levs + lax.axis_index("lev")
+
+
+def reduce_kernel(
+    sizes, factor, grad_ref, weight_ref, first_ref, second_ref,
+    new_weight_ref, new_first_ref, new_second_ref,
+    landed, piece, send_sems, recv_sems, out_sems, in_sems,
+):
+    count = sizes[0] * sizes[1] * sizes[2]
+    me = own_position(sizes)
+    barrier = pltpu.get_barrier_semaphore()
+
+    def greet(hop, carry):
+        peer = lax.rem(me + hop, count)
+        pl.semaphore_signal(barrier, inc=1, device_id=peer_at(peer, sizes), device_id_type=MESH)
+        return carry
+
+    lax.fori_loop(1, count, greet, 0)
+    pl.semaphore_wait(barrier, count - 1)
+
+    def share(hop):
+        peer = lax.rem(me + hop, count)
+        return pltpu.make_async_remote_copy(
+            src_ref=grad_ref.at[peer], dst_ref=landed.at[hop],
+            send_sem=send_sems.at[hop], recv_sem=recv_sems.at[hop],
+            device_id=peer_at(peer, sizes), device_id_type=MESH,
+        )
+
+    def spread(hop):
+        peer = lax.rem(me + hop, count)
+        return pltpu.make_async_remote_copy(
+            src_ref=piece, dst_ref=new_weight_ref.at[me],
+            send_sem=out_sems.at[hop], recv_sem=in_sems.at[hop],
+            device_id=peer_at(peer, sizes), device_id_type=MESH,
+        )
+
+    def start(make):
+        def body(hop, carry):
+            make(hop).start()
+            return carry
+        lax.fori_loop(1, count, body, 0)
+
+    start(share)
+
+    def add(hop, total):
+        share(hop).wait_recv()
+        return total + landed[hop]
+
+    total = lax.fori_loop(1, count, add, grad_ref[me])
+    piece[...], new_first_ref[...], new_second_ref[...] = adam_update(
+        weight_ref[me], total * factor, first_ref[...], second_ref[...]
+    )
+    start(spread)
+    new_weight_ref[me] = piece[...]
+
+    def arrive(hop, carry):
+        spread(hop).wait_recv()
+        return carry
+
+    def leave(hop, carry):
+        share(hop).wait_send()
+        spread(hop).wait_send()
+        return carry
+
+    lax.fori_loop(1, count, arrive, 0)
+    lax.fori_loop(1, count, leave, 0)
+
+
+def reduce_update(sizes, factor, grad, weight, first, second):
+    count = sizes[0] * sizes[1] * sizes[2]
+    rows, lanes = first.shape
+    vmem = pl.BlockSpec(memory_space=pltpu.VMEM)
+    dma = pltpu.SemaphoreType.DMA((count,))
+    new_weight, new_first, new_second = pl.pallas_call(
+        functools.partial(reduce_kernel, sizes, factor),
+        out_shape=[
+            jax.ShapeDtypeStruct((count, rows, lanes), jnp.float32),
+            jax.ShapeDtypeStruct((rows, lanes), jnp.float32),
+            jax.ShapeDtypeStruct((rows, lanes), jnp.float32),
+        ],
+        in_specs=[vmem] * 4,
+        out_specs=[vmem] * 3,
+        scratch_shapes=[
+            pltpu.VMEM((count, rows, lanes), jnp.float32),
+            pltpu.VMEM((rows, lanes), jnp.float32),
+            dma, dma, dma, dma,
+        ],
+        compiler_params=pltpu.CompilerParams(collective_id=1, has_side_effects=True),
+        name="reduce_update",
+    )(grad.reshape(count, rows, lanes), weight.reshape(count, rows, lanes), first, second)
+    return new_weight.reshape(count * rows, lanes), new_first, new_second
 
 
 def shards(
@@ -105,26 +233,27 @@
         d_input.reshape(col_shape), "lev", split_axis=0, concat_axis=1, tiled=True
     )
     input_cotangent = costate + d_levels.astype(jnp.float32)
-    part_in = part_in * factor
-    part_out = part_out * factor
-    share = mean_estimate_entry_matrix.shape[1]
-    leading_position = lax.axis_index(("col", "sec", "lev")) * share
-    grad_in, grad_out = (
-        lax.psum_scatter(part_in, ("col", "sec", "lev"), scatter_dimension=1, tiled=True),
-        lax.psum_scatter(part_out, ("col", "sec", "lev"), scatter_dimension=0, tiled=True),
-    )
-    own_in = lax.dynamic_slice_in_dim(entry_layer_matrix, leading_position, share, 1)
-    own_out = lax.dynamic_slice_in_dim(final_layer_matrix, leading_position, share, 0)
-    piece_in, new_first_in, new_second_in = adam_update(
-        own_in, grad_in, mean_estimate_entry_matrix, squared_estimate_entry_matrix
-    )
-    piece_out, new_first_out, new_second_out = adam_update(
-        own_out, grad_out, mean_estimate_final_matrix, squared_estimate_final_matrix
-    )
-    new_w_in, new_w_out = (
-        lax.all_gather(piece_in, ("col", "sec", "lev"), axis=1, tiled=True),
-        lax.all_gather(piece_out, ("col", "sec", "lev"), axis=0, tiled=True),
-    )
+    sizes = tuple(lax.axis_size(axis) for axis in REDUCED)
+    levs = sizes[2]
+
+    def packed(of_out, of_in):
+        return jnp.concatenate([slots(of_out, levs), slots(of_in.T, levs)], axis=1)
+
+    def unpacked(value):
+        half = value.shape[1] // 2
+        return (
+            unslots(value[:, half:], levs, levels_all).T,
+            unslots(value[:, :half], levs, levels_all),
+        )
+
+    new_weight, new_first, new_second = reduce_update(
+        sizes, factor, packed(part_out, part_in), packed(final_layer_matrix, entry_layer_matrix),
+        packed(mean_estimate_final_matrix, mean_estimate_entry_matrix),
+        packed(squared_estimate_final_matrix, squared_estimate_entry_matrix),
+    )
+    new_w_in, new_w_out = unpacked(new_weight)
+    new_first_in, new_first_out = unpacked(new_first)
+    new_second_in, new_second_out = unpacked(new_second)
     return (
         input_cotangent,
         new_w_in,

time: 269 us -> 153 us (0.57)
  waiting for transfers between devices: 90.2 us -> 0.03 us
  blocking collectives: 44.7 us -> 10.6 us
  Pallas kernels: 0 us -> 18.7 us
  between operations: 14.4 us -> 1.17 us
  local copies, waits for them, and re-layouts: 48 us -> 57.3 us
  starting transfers between devices: 24.1 us -> 20.1 us
  other arithmetic: 34.4 us -> 31.5 us
    reduce_scatter x1 -> x0, waiting for transfers between devices: 53.1 us -> none  [shards(): lax.psum_scatter(part_out, ('col', 'sec', 'lev'), scatter_dimension=0, ti...]
    all_gather x2 -> x0, blocking collectives: 39.5 us -> none  [the longest x1 19.7 us: shards(): lax.all_gather(piece_in, ('col', 'sec', 'lev'), axis=1, tiled=True)]
    unnamed x3 -> x0, waiting for transfers between devices: 35.9 us -> none
    pallas_call x0 -> x1, Pallas kernels: none -> 18.7 us  [reduce_update(): pl.pallas_call(functools.partial(reduce_kernel, sizes, factor), out_shape...]
    reshape x0 -> x20, local copies, waits for them, and re-layouts: none -> 6.35 us  [the longest x6 3.99 us: unslots(): return value.reshape(value.shape[0], levels_all)]
    all_to_all x0 -> x1, blocking collectives: none -> 5.2 us  [shards(): lax.all_to_all(thermal_departure, 'lev', split_axis=1, concat_axis=0, til...]
    all_to_all x1 -> x0, starting transfers between devices: 3.58 us -> none  [shards(): lax.all_to_all(thermal_departure, 'lev', split_axis=1, concat_axis=0, til...]
    dot_general x0 -> x2, local copies, waits for them, and re-layouts: none -> 3.53 us  [the longest x1 3.31 us: shards(): lax.dot_general(flat, d_pre, (((1,), (1,)), ((), ())), preferred_element_...]
  transfers between devices with their start and end apart: 16 -> 13, of which waited for: 3 -> 0; matrix products, arithmetic and copies ran while one was open for 19% -> 35% of each run, Pallas kernels for 0% -> 12%
where the time goes in v1:
time: 153 us; the launch traced here: 152 us
  local copies, waits for them, and re-layouts  57.3 us (37%)
  other arithmetic  31.5 us (21%)
  starting transfers between devices  20.1 us (13%)
  Pallas kernels  18.7 us (12%)
  matrix products  12.9 us (8%)
  blocking collectives  10.6 us (7%)
    add x3, other arithmetic, adjoint_step(): costate + zonal_flow_ratio * (next_x - costate)  20.1 us
    pallas_call x1, Pallas kernels, reduce_update(): pl.pallas_call(functools.partial(reduce_kernel, sizes, factor), out_shape...  18.7 us
    ppermute x8, starting transfers between devices, from_behind(): lax.ppermute(value, axis, [(source, source + steps) for source in range(f...  10.5 us
    slice x4, local copies, waits for them, and re-layouts, adjoint_step(): next_y = jnp.concatenate([costate[:, :, 1:], edge_y], axis=2)  7.52 us
    convert_element_type x1, other arithmetic, shards(): costate_bf = costate.astype(jnp.bfloat16)  6.76 us
    unnamed x39, local copies, waits for them, and re-layouts  6.41 us
    slice x4, local copies, waits for them, and re-layouts, adjoint_step(): next_x = jnp.concatenate([costate[:, 1:, :], edge_x], axis=1)  6.15 us
    ppermute x4, starting transfers between devices, passed_along(): return lax.ppermute(value, axis, pairs)  6.06 us
  transfers between devices with their start and end apart: 13, of which 0 were waited for; matrix products, arithmetic and copies ran while one was open for 35% of the time, Pallas kernels for 12%

profile of v1, /device:TPU:0, one launch (start us, length us, event | category | flops | bytes accessed | tf_op | source)
XLA Modules:
  0.0 152.3 jit_solution(10089612850709956891)
XLA Ops:
  1.8 5.1 %collective-permute-start = (f32[30,1,256]{2,1,0:T(1,128)S(1)}, f32[30,1,256]{2,1,0:T(1,128)S(1)}, u32[]{:S(2)}, u32[]{:S(2)}) collective-permute-start(f32[30,1,256]{2,1,0:T(1,128)S(1)} %slice.109), channel_id=1, source_target_pairs={{0,12},{4,0},{8,4},{12,8},{1,13},{5,1},{9,5},{13,9},{2,14},{6,2},{... | collective-permute-start | bytes 92168 | tf_op jit(solution)/shard_map/ppermute | solution.py:21
  11.2 5.2 %all_to_all.39 = bf16[30,64,256]{2,0,1:T(8,128)(2,1)S(1)} all-to-all(bf16[30,64,256]{2,0,1:T(8,128)(2,1)S(1)} %copy.133), channel_id=1, replica_groups=mesh['group'=2,'col'=4,'sec'=2,'lev'=2] {'lev'}, dimensions={1} | all-to-all | bytes 1966080 | tf_op jit(solution)/shard_map/all_to_all | solution.py:212
  17.8 4.7 %convolution_tanh_fusion = f32[256,8192]{0,1:T(8,128)} fusion(bf16[60,8192]{1,0:T(8,128)(2,1)S(1)} %bitcast.83, f32[60,256]{1,0:T(8,128)S(1)} %copy-done.7), kind=kOutput, calls=%fused_computation | convolution fusion | flops 251673600 | bytes 9433088 | tf_op jit(solution)/shard_map/dot_general | solution.py:216
  24.0 1.9 %slice.110 = f32[30,64,255]{2,1,0:T(8,128)} slice(f32[30,64,256]{2,1,0:T(8,128)S(1)} %copy-done.3), slice={[0:30], [0:64], [1:256]} | slice | bytes 3916800 | tf_op jit(solution)/shard_map/slice | solution.py:42
  29.8 6.9 %fusion.10 = f32[30,64,256]{2,1,0:T(8,128)S(1)} fusion(f32[30,64,256]{2,1,0:T(8,128)} %param.12, f32[30,64,256]{2,1,0:T(8,128)} %param.13, f32[30,1,256]{2,1,0:T(1,128)S(1)} %collective-permute-done, f32[30,63,256]{2,1,0:T(8,128)} %slice.108, f32[30,64,256]{2,1,0:T(8,128)} %param.14, f32[30,64,1]{2,1,0:T(8,128)} %copy.123, f32[30,64,255]{2,1,0:T(8,128)} %slice.110, ...), kind=kLoop, calls=%fused_computation.14 | loop fusion | flops 5898240 | bytes 15728640 | tf_op jit(solution)/shard_map/add | solution.py:45
  40.2 1.6 %copy.124 = f32[30,64,1]{1,0,2:T(8,128)S(1)} copy(f32[30,64,1]{2,1,0:T(8,128)} %slice.147) | data formatting | bytes 15360 | tf_op jit(solution)/shard_map/slice | solution.py:39
  46.9 1.9 %slice.146 = f32[30,64,255]{2,1,0:T(8,128)} slice(f32[30,64,256]{2,1,0:T(8,128)S(1)} %fusion.10), slice={[0:30], [0:64], [1:256]} | slice | bytes 3916800 | tf_op jit(solution)/shard_map/slice | solution.py:42
  48.8 1.6 %slice.144 = f32[30,63,256]{2,1,0:T(8,128)} slice(f32[30,64,256]{2,1,0:T(8,128)S(1)} %fusion.10), slice={[0:30], [1:64], [0:256]} | slice | bytes 3870720 | tf_op jit(solution)/shard_map/slice | solution.py:41
  50.4 2.1 %copy.125 = f32[30,64,1]{2,1,0:T(8,128)} copy(f32[30,64,1]{1,0,2:T(8,128)} %collective-permute-done.4) | data formatting | bytes 15360 | tf_op jit(solution)/shard_map/ppermute | solution.py:27
  52.5 6.9 %fusion.16 = f32[30,64,256]{2,1,0:T(8,128)S(1)} fusion(f32[30,64,256]{2,1,0:T(8,128)} %copy-done, f32[30,64,256]{2,1,0:T(8,128)} %param.13, f32[30,1,256]{2,1,0:T(1,128)} %collective-permute-done.3, f32[30,63,256]{2,1,0:T(8,128)} %slice.144, f32[30,64,256]{2,1,0:T(8,128)} %param.14, f32[30,64,1]{2,1,0:T(8,128)} %copy.125, f32[30,64,255]{2,1,0:T(8,128)} %slice.146, ...), kind=kLoop, calls=%fused_computation.23 | loop fusion | flops 5898240 | bytes 15728640 | tf_op jit(solution)/shard_map/add | solution.py:45
  62.2 1.6 %copy.126 = f32[30,64,1]{1,0,2:T(8,128)S(1)} copy(f32[30,64,1]{2,1,0:T(8,128)} %slice.153) | data formatting | bytes 15360 | tf_op jit(solution)/shard_map/slice | solution.py:39
  67.7 1.9 %slice.152 = f32[30,64,255]{2,1,0:T(8,128)} slice(f32[30,64,256]{2,1,0:T(8,128)S(1)} %fusion.16), slice={[0:30], [0:64], [1:256]} | slice | bytes 3916800 | tf_op jit(solution)/shard_map/slice | solution.py:42
  69.7 1.5 %slice.150 = f32[30,63,256]{2,1,0:T(8,128)} slice(f32[30,64,256]{2,1,0:T(8,128)S(1)} %fusion.16), slice={[0:30], [1:64], [0:256]} | slice | bytes 3870720 | tf_op jit(solution)/shard_map/slice | solution.py:41
  72.6 6.3 %fusion.22 = f32[30,64,256]{2,1,0:T(8,128)S(1)} fusion(f32[30,64,256]{2,1,0:T(8,128)S(1)} %fusion.16, f32[30,64,256]{2,1,0:T(8,128)} %param.13, f32[30,1,256]{2,1,0:T(1,128)S(1)} %collective-permute-done.6, f32[30,63,256]{2,1,0:T(8,128)} %slice.150, f32[30,64,256]{2,1,0:T(8,128)} %param.14, f32[30,64,1]{2,1,0:T(8,128)} %copy.127, f32[30,64,255]{2,1,0:T(8,128)} %slice.152, ...), kind=kLoop, calls=%fused_computation.32 | loop fusion | flops 5898240 | bytes 15728640 | tf_op jit(solution)/shard_map/add | solution.py:45
  84.0 1.5 %copy.171 = bf16[30,2,32,256]{3,2,1,0:T(8,128)(2,1)} copy(bf16[30,2,32,256]{3,0,2,1:T(8,128)(2,1)S(1)} %bitcast.79) | data formatting | bytes 1966080 | tf_op jit(solution)/shard_map/all_to_all | solution.py:212
  85.6 3.3 %dot_general.27 = bf16[2,30,8192]{2,0,1:T(2,128)(2,1)} reshape(bf16[2,30,32,256]{3,2,0,1:T(8,128)(2,1)} %bitcast.91) | data formatting | bytes 1966080 | tf_op jit(solution)/shard_map/dot_general | solution.py:228
  90.3 1.8 %slice.158 = f32[30,64,255]{2,1,0:T(8,128)} slice(f32[30,64,256]{2,1,0:T(8,128)S(1)} %copy-done.2), slice={[0:30], [0:64], [1:256]} | slice | bytes 3916800 | tf_op jit(solution)/shard_map/slice | solution.py:42
  92.1 1.5 %slice.156 = f32[30,63,256]{2,1,0:T(8,128)} slice(f32[30,64,256]{2,1,0:T(8,128)S(1)} %copy-done.2), slice={[0:30], [1:64], [0:256]} | slice | bytes 3870720 | tf_op jit(solution)/shard_map/slice | solution.py:41
  94.1 6.8 %fusion.36 = (bf16[30,64,256]{2,1,0:T(8,128)(2,1)S(1)}, f32[30,64,256]{2,1,0:T(8,128)}) fusion(f32[30,64,256]{2,1,0:T(8,128)} %param.15, f32[30,64,256]{2,1,0:T(8,128)S(1)} %copy-done.2, f32[1,64,256]{2,1,0:T(8,128)S(1)} %collective-permute-done.11, f32[29,64,256]{2,1,0:T(8,128)} %slice.160, f32[30,64,256]{2,1,0:T(8,128)} %param.14, ...), kind=kLoop, calls=%fused_computation.59 | loop fusion | flops 6389760 | bytes 16711680 | tf_op jit(solution)/shard_map/convert_element_type | solution.py:210
  101.4 5.4 %all_to_all.40 = bf16[30,64,256]{2,0,1:T(8,128)(2,1)S(1)} all-to-all(bf16[30,64,256]{2,0,1:T(8,128)(2,1)S(1)} %copy.130), channel_id=1, replica_groups=mesh['group'=2,'col'=4,'sec'=2,'lev'=2] {'lev'}, dimensions={1} | all-to-all | bytes 1966080 | tf_op jit(solution)/shard_map/all_to_all | solution.py:213
  108.9 4.5 %fusion.4 = f32[256,2,30]{0,2,1:T(8,128)S(1)} fusion(f32[256,8192]{0,1:T(8,128)} %convolution_tanh_fusion, bf16[2,30,8192]{2,0,1:T(2,128)(2,1)S(1)} %dot_general.25), kind=kOutput, calls=%fused_computation.7 | convolution fusion | flops 253755392 | bytes 9433088 | tf_op jit(solution)/shard_map/dot_general | solution.py:223
  118.6 3.6 %all-to-all-start.2 = ((bf16[60,32,256]{2,1,0:T(8,128)(2,1)}), bf16[60,32,256]{2,1,0:T(8,128)(2,1)S(1)}, u32[]{:S(2)}, u32[]{:S(2)}) async-start(bf16[60,32,256]{2,1,0:T(8,128)(2,1)} %slice.170), calls=%async_computation.2 | async-start | bytes 1966080 | tf_op jit(solution)/shard_map/all_to_all | solution.py:232
  123.9 18.7 %reduce_update.1 = (f32[16,16,128]{2,1,0:T(8,128)}, f32[16,128]{1,0:T(8,128)}, f32[16,128]{1,0:T(8,128)}) custom-call(f32[16,16,128]{2,1,0:T(8,128)} %pad_maximum_fusion.grad_ref, f32[16,16,128]{2,1,0:T(8,128)} %pad_maximum_fusion.1.weight_ref, f32[16,128]{1,0:T(8,128)} %pad_maximum_fusion.2.first_ref, f32[16,128]{1,0:T(8,128)} %pad_maximum_fusion.3.second_ref), custom_call_target="tpu_custom_call" | custom-call | tf_op jit(solution)/shard_map/reduce_update/pallas_call | solution.py:164
  150.8 1.5 %bitcast_add_fusion = f32[30,64,256]{2,1,0:T(8,128)} fusion(f32[30,64,256]{2,1,0:T(8,128)S(1)} %copy-done.4, f32[30,2,32,256]{3,2,1,0:T(8,128)S(1)} %copy.137), kind=kLoop, calls=%fused_computation.47 | loop fusion | flops 491520 | bytes 5898240 | tf_op jit(solution)/shard_map/add | solution.py:235
  (135 shorter events, 53.3 us)
Async XLA Ops:
  0.6 8.4 %slice-start.2 = ((f32[30,64,256]{2,1,0:T(8,128)}), f32[30,64,1]{2,1,0:T(8,128)S(1)}, s32[]{:S(2)}) async-start(f32[30,64,256]{2,1,0:T(8,128)} %param.12), calls=%async_computation.5 | async-start | bytes 1966080 | tf_op jit(solution)/shard_map/slice | solution.py:39
  0.6 10.0 %copy-start.5 = (bf16[30,64,256]{2,1,0:T(8,128)(2,1)S(1)}, bf16[30,64,256]{2,1,0:T(8,128)(2,1)}, u32[]{:S(2)}) copy-start(bf16[30,64,256]{2,1,0:T(8,128)(2,1)} %param.11) | copy-start | bytes 2949124
  1.8 28.0 %collective-permute-start = (f32[30,1,256]{2,1,0:T(1,128)S(1)}, f32[30,1,256]{2,1,0:T(1,128)S(1)}, u32[]{:S(2)}, u32[]{:S(2)}) collective-permute-start(f32[30,1,256]{2,1,0:T(1,128)S(1)} %slice.109), channel_id=1, source_target_pairs={{0,12},{4,0},{8,4},{12,8},{1,13},{5,1},{9,5},{13,9},{2,14},{6,2},{... | collective-permute-start | bytes 92168 | tf_op jit(solution)/shard_map/ppermute | solution.py:21
  7.7 22.0 %collective-permute-start.2 = (f32[1,64,256]{2,1,0:T(8,128)S(1)}, f32[1,64,256]{2,1,0:T(8,128)S(1)}, u32[]{:S(2)}, u32[]{:S(2)}) collective-permute-start(f32[1,64,256]{2,1,0:T(8,128)S(1)} %slice.113), channel_id=1, source_target_pairs={{1,0},{3,2},{5,4},{7,6},{9,8},{11,10},{13,12},{15,14},{17,16},{19,... | collective-permute-start | bytes 196616 | tf_op jit(solution)/shard_map/ppermute | solution.py:27
  9.4 19.0 %collective-permute-start.1 = (f32[30,64,1]{1,0,2:T(8,128)S(1)}, f32[30,64,1]{1,0,2:T(8,128)S(1)}, u32[]{:S(2)}, u32[]{:S(2)}) collective-permute-start(f32[30,64,1]{1,0,2:T(8,128)S(1)} %copy.155), channel_id=1, source_target_pairs={{2,0},{3,1},{6,4},{7,5},{10,8},{11,9},{14,12},{15,13},{18,16},{19,... | collective-permute-start | bytes 23048 | tf_op jit(solution)/shard_map/ppermute | solution.py:27
  17.8 4.7 %copy-start.3 = (f32[30,64,256]{2,1,0:T(8,128)S(1)}, f32[30,64,256]{2,1,0:T(8,128)}, u32[]{:S(2)}) copy-start(f32[30,64,256]{2,1,0:T(8,128)} %param.12) | copy-start | bytes 5898244
  25.9 1.5 copy-start.8
  36.6 12.2 %copy-start = (f32[30,64,256]{2,1,0:T(8,128)}, f32[30,64,256]{2,1,0:T(8,128)S(1)}, u32[]{:S(2)}) copy-start(f32[30,64,256]{2,1,0:T(8,128)S(1)} %fusion.10) | copy-start | bytes 5898244
  38.4 14.1 %collective-permute-start.3 = (f32[30,1,256]{2,1,0:T(1,128)}, f32[30,1,256]{2,1,0:T(1,128)}, u32[]{:S(2)}, u32[]{:S(2)}) collective-permute-start(f32[30,1,256]{2,1,0:T(1,128)} %slice.145), channel_id=1, source_target_pairs={{0,12},{4,0},{8,4},{12,8},{1,13},{5,1},{9,5},{13,9},{2,14},{6,2},{... | collective-permute-start | bytes 92168 | tf_op jit(solution)/shard_map/ppermute | solution.py:21
  38.9 13.6 %collective-permute-start.5 = (f32[1,64,256]{2,1,0:T(8,128)S(1)}, f32[1,64,256]{2,1,0:T(8,128)S(1)}, u32[]{:S(2)}, u32[]{:S(2)}) collective-permute-start(f32[1,64,256]{2,1,0:T(8,128)S(1)} %slice.149), channel_id=1, source_target_pairs={{1,0},{3,2},{5,4},{7,6},{9,8},{11,10},{13,12},{15,14},{17,16},{19,... | collective-permute-start | bytes 196616 | tf_op jit(solution)/shard_map/ppermute | solution.py:27
  41.7 8.7 %collective-permute-start.4 = (f32[30,64,1]{1,0,2:T(8,128)S(1)}, f32[30,64,1]{1,0,2:T(8,128)}, u32[]{:S(2)}, u32[]{:S(2)}) collective-permute-start(f32[30,64,1]{1,0,2:T(8,128)S(1)} %copy.124), channel_id=1, source_target_pairs={{2,0},{3,1},{6,4},{7,5},{10,8},{11,9},{14,12},{15,13},{18,16},{19,... | collective-permute-start | bytes 23048 | tf_op jit(solution)/shard_map/ppermute | solution.py:27
  59.4 6.6 %copy-start.9 = (f32[60,16]{0,1:T(8,128)S(1)}, f32[60,16]{0,1:T(8,128)}, u32[]{:S(2)}) copy-start(f32[60,16]{0,1:T(8,128)} %param.19) | copy-start | bytes 11524
  59.4 6.7 %copy-start.10 = (f32[16,60]{1,0:T(8,128)S(1)}, f32[16,60]{1,0:T(8,128)}, u32[]{:S(2)}) copy-start(f32[16,60]{1,0:T(8,128)} %param.21) | copy-start | bytes 11524
  60.5 12.1 %collective-permute-start.6 = (f32[30,1,256]{2,1,0:T(1,128)S(1)}, f32[30,1,256]{2,1,0:T(1,128)S(1)}, u32[]{:S(2)}, u32[]{:S(2)}) collective-permute-start(f32[30,1,256]{2,1,0:T(1,128)S(1)} %slice.151), channel_id=1, source_target_pairs={{0,12},{4,0},{8,4},{12,8},{1,13},{5,1},{9,5},{13,9},{2,14},{6,2},{... | collective-permute-start | bytes 92168 | tf_op jit(solution)/shard_map/ppermute | solution.py:21
  60.9 11.7 %collective-permute-start.8 = (f32[1,64,256]{2,1,0:T(8,128)S(1)}, f32[1,64,256]{2,1,0:T(8,128)S(1)}, u32[]{:S(2)}, u32[]{:S(2)}) collective-permute-start(f32[1,64,256]{2,1,0:T(8,128)S(1)} %slice.155), channel_id=1, source_target_pairs={{1,0},{3,2},{5,4},{7,6},{9,8},{11,10},{13,12},{15,14},{17,16},{19,... | collective-permute-start | bytes 196616 | tf_op jit(solution)/shard_map/ppermute | solution.py:27
  63.8 7.4 %collective-permute-start.7 = (f32[30,64,1]{1,0,2:T(8,128)S(1)}, f32[30,64,1]{1,0,2:T(8,128)S(1)}, u32[]{:S(2)}, u32[]{:S(2)}) collective-permute-start(f32[30,64,1]{1,0,2:T(8,128)S(1)} %copy.126), channel_id=1, source_target_pairs={{2,0},{3,1},{6,4},{7,5},{10,8},{11,9},{14,12},{15,13},{18,16},{19,... | collective-permute-start | bytes 23048 | tf_op jit(solution)/shard_map/ppermute | solution.py:27
  80.3 13.8 %collective-permute-start.9 = (f32[30,1,256]{2,1,0:T(1,128)S(1)}, f32[30,1,256]{2,1,0:T(1,128)S(1)}, u32[]{:S(2)}, u32[]{:S(2)}) collective-permute-start(f32[30,1,256]{2,1,0:T(1,128)S(1)} %slice.157), channel_id=1, source_target_pairs={{0,12},{4,0},{8,4},{12,8},{1,13},{5,1},{9,5},{13,9},{2,14},{6,2},{... | collective-permute-start | bytes 92168 | tf_op jit(solution)/shard_map/ppermute | solution.py:21
  80.4 13.7 %collective-permute-start.11 = (f32[1,64,256]{2,1,0:T(8,128)S(1)}, f32[1,64,256]{2,1,0:T(8,128)S(1)}, u32[]{:S(2)}, u32[]{:S(2)}) collective-permute-start(f32[1,64,256]{2,1,0:T(8,128)S(1)} %slice.161), channel_id=1, source_target_pairs={{1,0},{3,2},{5,4},{7,6},{9,8},{11,10},{13,12},{15,14},{17,16},{19,... | collective-permute-start | bytes 196616 | tf_op jit(solution)/shard_map/ppermute | solution.py:27
  82.0 11.7 %collective-permute-start.10 = (f32[30,64,1]{1,0,2:T(8,128)S(1)}, f32[30,64,1]{1,0,2:T(8,128)S(1)}, u32[]{:S(2)}, u32[]{:S(2)}) collective-permute-start(f32[30,64,1]{1,0,2:T(8,128)S(1)} %copy.128), channel_id=1, source_target_pairs={{2,0},{3,1},{6,4},{7,5},{10,8},{11,9},{14,12},{15,13},{18,16},{19,... | collective-permute-start | bytes 23048 | tf_op jit(solution)/shard_map/ppermute | solution.py:27
  84.0 4.9 %copy-start.2 = (f32[30,64,256]{2,1,0:T(8,128)S(1)}, f32[30,64,256]{2,1,0:T(8,128)}, u32[]{:S(2)}) copy-start(f32[30,64,256]{2,1,0:T(8,128)} %copy-done.1) | copy-start | bytes 5898244
  107.6 5.8 %slice-start = ((s8[8388608]{0:T(1024)(128)(4,1)}), s8[4194304]{0:T(1024)(128)(4,1)S(1)}, s32[]{:S(2)}) async-start(s8[8388608]{0:T(1024)(128)(4,1)} %bitcast.76), calls=%async_computation.3 | async-start | bytes 8388608
  108.9 4.8 %slice-start.1 = ((s8[8388608]{0:T(1024)(128)(4,1)}), s8[4194304]{0:T(1024)(128)(4,1)S(1)}, s32[]{:S(2)}) async-start(s8[8388608]{0:T(1024)(128)(4,1)} %bitcast.76), calls=%async_computation.4 | async-start | bytes 8388608
  118.6 30.4 %all-to-all-start.2 = ((bf16[60,32,256]{2,1,0:T(8,128)(2,1)}), bf16[60,32,256]{2,1,0:T(8,128)(2,1)S(1)}, u32[]{:S(2)}, u32[]{:S(2)}) async-start(bf16[60,32,256]{2,1,0:T(8,128)(2,1)} %slice.170), calls=%async_computation.2 | async-start | bytes 1966080 | tf_op jit(solution)/shard_map/all_to_all | solution.py:232
  149.3 1.6 %copy-start.4 = (f32[30,64,256]{2,1,0:T(8,128)S(1)}, f32[30,64,256]{2,1,0:T(8,128)}, u32[]{:S(2)}) copy-start(f32[30,64,256]{2,1,0:T(8,128)} %get-tuple-element.21) | copy-start | bytes 5898244
  (3 other events, 3.5 us)

commit v2 on v1

--- a/solution.py
+++ b/solution.py
@@ -15,45 +15,11 @@
 bias_second = 1.0 - 0.999**10
 
 
-def passed_along(value, axis, steps):
-    count = lax.axis_size(axis)
-    pairs = [(source, (source + steps) % count) for source in range(count)]
-    return lax.ppermute(value, axis, pairs)
-
-
-def from_behind(value, axis, steps):
-    count = lax.axis_size(axis)
-    first, last = (max(0, -steps), min(count, count - steps))
-    return lax.ppermute(value, axis, [(source, source + steps) for source in range(first, last)])
-
-
 def adam_update(weight, grad, first, second):
     new_first = 0.9 * first + 0.1 * grad
     new_second = 0.999 * second + 0.001 * grad * grad
     step_size = new_first / bias_first / (jnp.sqrt(new_second / bias_second) + 1e-08)
     return (weight - 0.01 * step_size, new_first, new_second)
-
-
-def adjoint_step(costate, zonal_flow_ratio, meridional_flow_ratio, updraft_flow_ratio):
-    edge_x = passed_along(costate[:, 0:1, :], "col", -1)
-    edge_y = from_behind(costate[:, :, 0:1], "sec", -1)
-    edge_z = from_behind(costate[0:1], "lev", -1)
-    next_x = jnp.concatenate([costate[:, 1:, :], edge_x], axis=1)
-    next_y = jnp.concatenate([costate[:, :, 1:], edge_y], axis=2)
-    next_z = jnp.concatenate([costate[1:], edge_z], axis=0)
-    return (
-        costate
-        + zonal_flow_ratio * (next_x - costate)
-        + meridional_flow_ratio * (next_y - costate)
-        + updraft_flow_ratio * (next_z - costate)
-    )
-
-
-def transport(seed_sensitivity, zonal_flow_ratio, meridional_flow_ratio, updraft_flow_ratio):
-    costate = seed_sensitivity
-    for step in range(STEPS):
-        costate = adjoint_step(costate, zonal_flow_ratio, meridional_flow_ratio, updraft_flow_ratio)
-    return costate
 
 
 MESH = pl.DeviceIdType.MESH
@@ -181,6 +147,386 @@
     return new_weight.reshape(count * rows, lanes), new_first, new_second
 
 
+def halves(levels):
+    first = -(-levels // 16) * 8
+    return ((0, first), (first, levels))
+
+
+def column_kernel(
+    sizes, theta_hbm, seed_hbm, zonal_hbm, merid_hbm, updraft_hbm, weight_ref,
+    out_hbm, grad_ref,
+    v, zonal, merid, updraft, edge_x, halo_x, edge_y, halo_y, edge_z, halo_z,
+    theta_own, theta_far, profile, back_far, d_in, d_far, w_out, w_in, w_in_t,
+    load_sems, seed_sems, theta_sems, x_sems, y_sems, z_sems, back_sems, d_sems, out_sems,
+):
+    cols, secs, _ = sizes
+    levels, rows, lanes = seed_hbm.shape
+    slot = v.shape[1]
+    pieces = lanes // 128
+    half = rows // 2
+    col, sec, lev = (lax.axis_index(axis) for axis in REDUCED)
+    other = 1 - lev
+    own_row = pl.multiple_of(lev * half, half)
+    far_row = pl.multiple_of(other * half, half)
+    own_slot = lev * slot
+    far_slot = other * slot
+    parts = halves(levels)
+    col_before = lax.rem(col + cols - 1, cols)
+    col_after = lax.rem(col + 1, cols)
+
+    theta_in = pltpu.make_async_copy(
+        theta_hbm.at[:, pl.ds(own_row, half), :], theta_own, theta_sems.at[0]
+    )
+    loads, seeds = [], []
+    for part, (low, high) in enumerate(parts):
+        span = pl.ds(low, high - low)
+        loads.append([
+            pltpu.make_async_copy(source.at[span], target.at[span], load_sems.at[at, part])
+            for at, (source, target) in enumerate(
+                ((zonal_hbm, zonal), (merid_hbm, merid), (updraft_hbm, updraft))
+            )
+        ])
+        seeds.append([
+            pltpu.make_async_copy(
+                seed_hbm.at[span, :, pl.ds(128 * piece, 128)], v.at[piece, span],
+                seed_sems.at[piece, part],
+            )
+            for piece in range(pieces)
+        ])
+    for group in seeds + loads:
+        for copy in group:
+            copy.start()
+    theta_in.start()
+
+    barrier = pltpu.get_barrier_semaphore()
+    pl.semaphore_signal(barrier, inc=1, device_id={"col": col_before}, device_id_type=MESH)
+    pl.semaphore_signal(barrier, inc=1, device_id={"col": col_after}, device_id_type=MESH)
+    pl.semaphore_signal(barrier, inc=1, device_id={"lev": other}, device_id_type=MESH)
+
+    @pl.when(sec > 0)
+    def _():
+        pl.semaphore_signal(barrier, inc=1, device_id={"sec": sec - 1}, device_id_type=MESH)
+
+    @pl.when(sec < secs - 1)
+    def _():
+        pl.semaphore_signal(barrier, inc=1, device_id={"sec": sec + 1}, device_id_type=MESH)
+
+    @pl.when(sec == secs - 1)
+    def _():
+        halo_y[...] = jnp.zeros_like(halo_y)
+
+    @pl.when(lev == 1)
+    def _():
+        halo_z[...] = jnp.zeros_like(halo_z)
+
+    pl.semaphore_wait(
+        barrier, 3 + (sec > 0).astype(jnp.int32) + (sec < secs - 1).astype(jnp.int32)
+    )
+
+    theta_out = pltpu.make_async_remote_copy(
+        src_ref=theta_hbm.at[:, pl.ds(far_row, half), :], dst_ref=theta_far,
+        send_sem=theta_sems.at[1], recv_sem=theta_sems.at[2],
+        device_id={"lev": other}, device_id_type=MESH,
+    )
+    theta_out.start()
+
+    def x_copy(step, part):
+        low, high = parts[part]
+        span = pl.ds(low, slot - low if part else high)
+        return pltpu.make_async_remote_copy(
+            src_ref=edge_x.at[step, span], dst_ref=halo_x.at[step, span],
+            send_sem=x_sems.at[0, step, part], recv_sem=x_sems.at[1, step, part],
+            device_id={"col": col_before}, device_id_type=MESH,
+        )
+
+    def y_copy(step, part):
+        return pltpu.make_async_remote_copy(
+            src_ref=edge_y.at[step, part], dst_ref=halo_y.at[step, part],
+            send_sem=y_sems.at[0, step, part], recv_sem=y_sems.at[1, step, part],
+            device_id={"sec": jnp.maximum(sec - 1, 0)}, device_id_type=MESH,
+        )
+
+    def z_copy(step):
+        return pltpu.make_async_remote_copy(
+            src_ref=edge_z.at[step], dst_ref=halo_z.at[step],
+            send_sem=z_sems.at[0, step], recv_sem=z_sems.at[1, step],
+            device_id={"lev": 0}, device_id_type=MESH,
+        )
+
+    def back_copy(part):
+        low, high = parts[part]
+        span = pl.ds(low, high - low)
+        return pltpu.make_async_remote_copy(
+            src_ref=v.at[:, span, pl.ds(far_row, half), :], dst_ref=back_far.at[:, span],
+            send_sem=back_sems.at[0, part], recv_sem=back_sems.at[1, part],
+            device_id={"lev": other}, device_id_type=MESH,
+        )
+
+    def whole(ref, z, span=slice(None)):
+        return jnp.concatenate([ref[piece, z, span, :] for piece in range(pieces)], axis=1)
+
+    def lay(ref, z, value):
+        for piece in range(pieces):
+            ref[piece, z] = value[:, 128 * piece : 128 * piece + 128]
+
+    tiles = rows // 8
+    lane = lax.broadcasted_iota(jnp.int32, (8, 128), 1)
+    last_lane = lax.broadcasted_iota(jnp.int32, (rows, lanes), 1) == lanes - 1
+    last_row = lax.broadcasted_iota(jnp.int32, (rows, lanes), 0) == rows - 1
+
+    def keep_edges(value, z, low, step, packed):
+        edge_x[step, pl.ds(z, 1), :] = value[0:1]
+        for tile in range(tiles):
+            packed = jnp.where(
+                lane == (z - low) * tiles + tile, value[8 * tile : 8 * tile + 8, 0:1], packed
+            )
+        return packed
+
+    def send_edges(step, part, packed):
+        edge_y[step, part] = packed
+        x_copy(step, part).start()
+
+        @pl.when(sec > 0)
+        def _():
+            y_copy(step, part).start()
+
+        if part == 0:
+            edge_z[step] = whole(v, 0)
+
+            @pl.when(lev == 1)
+            def _():
+                z_copy(step).start()
+
+    def advance(z, low, step, part, above):
+        now = whole(v, z)
+        strip = pltpu.roll(halo_y[step, part], lax.rem(128 - (z - low) * tiles, 128), axis=1)
+        column = jnp.concatenate([strip[:, tile : tile + 1] for tile in range(tiles)], axis=0)
+        next_x = jnp.where(last_row, halo_x[step, pl.ds(z, 1), :], pltpu.roll(now, rows - 1, axis=0))
+        next_y = jnp.where(last_lane, column, pltpu.roll(now, lanes - 1, axis=1))
+        new = (
+            now + zonal[z] * (next_x - now) + merid[z] * (next_y - now) + updraft[z] * (above - now)
+        )
+        lay(v, z, new)
+        return new
+
+    nothing = jnp.zeros((8, 128), jnp.float32)
+    for part, (low, high) in enumerate(parts):
+        for copy in seeds[part]:
+            copy.wait()
+        packed = lax.fori_loop(
+            low, high, lambda z, packed: keep_edges(whole(v, z), z, low, 0, packed), nothing
+        )
+        send_edges(0, part, packed)
+
+    weights = weight_ref[...]
+    middle = weights.shape[1] // 2
+    w_out[...] = weights[:, :middle].astype(jnp.bfloat16)
+    w_in[...] = weights[:, middle:].astype(jnp.bfloat16)
+    w_in_t[...] = weights[:, middle:].T.astype(jnp.bfloat16)
+    v[:, levels:] = jnp.zeros((pieces, slot - levels, rows, 128), jnp.float32)
+    back_far[:, levels:] = jnp.zeros((pieces, slot - levels, half, 128), jnp.float32)
+    for start in (levels, slot + levels):
+        profile[:, start : start + slot - levels] = jnp.zeros(
+            (pieces, slot - levels, half, 128), jnp.float32
+        )
+    theta_in.wait()
+
+    def widen(source, first):
+        def body(z, carry):
+            lay(profile, first + z, source[z].astype(jnp.float32))
+            return carry
+        lax.fori_loop(0, levels, body, 0)
+
+    widen(theta_own, own_slot)
+
+    for step in range(STEPS):
+        for part, (low, high) in enumerate(parts):
+            if step == 0:
+                for copy in loads[part]:
+                    copy.wait()
+            x_copy(step, part).wait_recv()
+
+            @pl.when(sec < secs - 1)
+            def _():
+                y_copy(step, part).wait_recv()
+
+            more = step + 1 < STEPS
+            inner = high if part == 0 else high - 1
+
+            def body(z, packed):
+                new = advance(z, low, step, part, whole(v, z + 1))
+                return keep_edges(new, z, low, step + 1, packed) if more else packed
+
+            packed = lax.fori_loop(low, inner, body, nothing)
+            if part == 1:
+
+                @pl.when(lev == 0)
+                def _():
+                    z_copy(step).wait_recv()
+
+                new = advance(inner, low, step, part, halo_z[step])
+                if more:
+                    packed = keep_edges(new, inner, low, step + 1, packed)
+            if more:
+                send_edges(step + 1, part, packed)
+            else:
+                back_copy(part).start()
+
+    theta_out.wait_recv()
+    widen(theta_far, far_slot)
+    for part in range(2):
+        back_copy(part).wait_recv()
+
+    grad_ref[...] = jnp.zeros_like(grad_ref)
+    v_rows = v.reshape(pieces * slot * rows, 128)
+    far_rows = back_far.reshape(pieces * slot * half, 128)
+    profile_rows = profile.reshape(pieces * 2 * slot * half, 128)
+    d_rows = d_in.reshape(pieces * 2 * slot * half, 128)
+    chunk, batch = 8, 4
+    places = [(row, piece) for row in range(batch) for piece in range(pieces)]
+
+    def d_copy(at):
+        span = pl.ds(pl.multiple_of(at * chunk, chunk), chunk)
+        return pltpu.make_async_remote_copy(
+            src_ref=d_in.at[:, pl.ds(far_slot, levels), span, :],
+            dst_ref=d_far.at[:, :, span, :],
+            send_sem=d_sems.at[0, at], recv_sem=d_sems.at[1, at],
+            device_id={"lev": other}, device_id_type=MESH,
+        )
+
+    def out_copy(at, side):
+        first = own_row if side == 0 else far_row
+        span = pl.ds(pl.multiple_of(first + at * chunk, chunk), chunk)
+        return pltpu.make_async_copy(
+            zonal.at[:, span, :], out_hbm.at[:, span, :], out_sems.at[side, at]
+        )
+
+    nt = (((1,), (1,)), ((), ()))
+
+    def network(at, carry):
+        for sub in range(chunk // batch):
+            first = at * chunk + sub * batch
+            x_parts, b_parts = [], []
+            for row, piece in places:
+                r = first + row
+                x_parts.append(
+                    profile_rows[pl.ds(piece * 2 * slot * half + r, 2 * slot, stride=half), :].astype(jnp.bfloat16)
+                )
+                own = v_rows[pl.ds(piece * slot * rows + own_row + r, slot, stride=rows), :]
+                far = far_rows[pl.ds(piece * slot * half + r, slot, stride=half), :]
+                low_half = jnp.where(lev == 0, own, far)
+                high_half = jnp.where(lev == 0, far, own)
+                b_parts.append(
+                    jnp.concatenate([low_half, high_half], axis=0).astype(jnp.bfloat16)
+                )
+            flat = jnp.concatenate(x_parts, axis=1)
+            back = jnp.concatenate(b_parts, axis=1)
+            act = jnp.tanh(jnp.dot(w_in[...], flat, preferred_element_type=jnp.float32))
+            d_act = jnp.dot(w_out[...], back, preferred_element_type=jnp.float32)
+            d_pre = (d_act * (1.0 - act * act)).astype(jnp.bfloat16)
+            of_out = lax.dot_general(
+                act.astype(jnp.bfloat16), back, nt, preferred_element_type=jnp.float32
+            )
+            of_in = lax.dot_general(d_pre, flat, nt, preferred_element_type=jnp.float32)
+            grad_ref[...] += jnp.concatenate([of_out, of_in], axis=1)
+            d_input = jnp.dot(w_in_t[...], d_pre, preferred_element_type=jnp.float32)
+            d_input = d_input.astype(jnp.bfloat16).astype(jnp.float32)
+            for at_place, (row, piece) in enumerate(places):
+                start = piece * 2 * slot * half + first + row
+                d_rows[pl.ds(start, 2 * slot, stride=half), :] = (
+                    d_input[:, at_place * 128 : at_place * 128 + 128]
+                )
+        d_copy(at).start()
+        span = pl.ds(pl.multiple_of(at * chunk, chunk), chunk)
+        own_span = pl.ds(pl.multiple_of(own_row + at * chunk, chunk), chunk)
+
+        def body(z, carry):
+            zonal[z, own_span, :] = whole(v, z, own_span) + whole(d_in, own_slot + z, span)
+            return carry
+
+        lax.fori_loop(0, levels, body, 0, unroll=5 if levels % 5 == 0 else 1)
+        out_copy(at, 0).start()
+        return carry
+
+    chunks = half // chunk
+    lax.fori_loop(0, chunks, network, 0)
+    def finish(at, carry):
+        d_copy(at).wait_recv()
+        span = pl.ds(pl.multiple_of(at * chunk, chunk), chunk)
+        far_span = pl.ds(pl.multiple_of(far_row + at * chunk, chunk), chunk)
+
+        def body(z, carry):
+            zonal[z, far_span, :] = whole(v, z, far_span) + whole(d_far, z, span)
+            return carry
+
+        lax.fori_loop(0, levels, body, 0, unroll=5 if levels % 5 == 0 else 1)
+        out_copy(at, 1).start()
+        return carry
+
+    lax.fori_loop(0, chunks, finish, 0)
+
+    def drain(at, carry):
+        d_copy(at).wait_send()
+        out_copy(at, 0).wait()
+        out_copy(at, 1).wait()
+        return carry
+
+    lax.fori_loop(0, chunks, drain, 0)
+    theta_out.wait_send()
+    for part in range(2):
+        back_copy(part).wait_send()
+    for step in range(STEPS):
+        for part in range(2):
+            x_copy(step, part).wait_send()
+
+            @pl.when(sec > 0)
+            def _():
+                y_copy(step, part).wait_send()
+
+        @pl.when(lev == 1)
+        def _():
+            z_copy(step).wait_send()
+
+
+def columns_back(sizes, theta, seed, zonal, merid, updraft, weight):
+    levels, rows, lanes = seed.shape
+    hidden, width = weight.shape
+    slot, half, pieces = width // 4, rows // 2, lanes // 128
+    f32, bf16 = jnp.float32, jnp.bfloat16
+    hbm = pl.BlockSpec(memory_space=pl.ANY)
+    vmem = pl.BlockSpec(memory_space=pltpu.VMEM)
+    dma = pltpu.SemaphoreType.DMA
+    ratio = pltpu.VMEM((levels, rows, lanes), f32)
+    return pl.pallas_call(
+        functools.partial(column_kernel, sizes),
+        out_shape=[
+            jax.ShapeDtypeStruct((levels, rows, lanes), f32),
+            jax.ShapeDtypeStruct((hidden, width), f32),
+        ],
+        in_specs=[hbm] * 5 + [vmem],
+        out_specs=[hbm, vmem],
+        scratch_shapes=[
+            pltpu.VMEM((pieces, slot, rows, 128), f32), ratio, ratio, ratio,
+            pltpu.VMEM((STEPS, slot, lanes), f32), pltpu.VMEM((STEPS, slot, lanes), f32),
+            pltpu.VMEM((STEPS, 2, 8, 128), f32), pltpu.VMEM((STEPS, 2, 8, 128), f32),
+            pltpu.VMEM((STEPS, rows, lanes), f32), pltpu.VMEM((STEPS, rows, lanes), f32),
+            pltpu.VMEM((levels, half, lanes), bf16), pltpu.VMEM((levels, half, lanes), bf16),
+            pltpu.VMEM((pieces, 2 * slot, half, 128), f32),
+            pltpu.VMEM((pieces, slot, half, 128), f32),
+            pltpu.VMEM((pieces, 2 * slot, half, 128), f32),
+            pltpu.VMEM((pieces, levels, half, 128), f32),
+            pltpu.VMEM((hidden, width // 2), bf16), pltpu.VMEM((hidden, width // 2), bf16),
+            pltpu.VMEM((width // 2, hidden), bf16),
+            dma((3, 2)), dma((pieces, 2)), dma((3,)), dma((2, STEPS, 2)), dma((2, STEPS, 2)), dma((2, STEPS)),
+            dma((2, 2)), dma((2, half // 8)), dma((2, half // 8)),
+        ],
+        compiler_params=pltpu.CompilerParams(
+            collective_id=2, has_side_effects=True, vmem_limit_bytes=48 * 1024 * 1024
+        ),
+        name="columns_back",
+    )(theta, seed, zonal, merid, updraft, weight)
+
+
 def shards(
     thermal_departure,
     seed_sensitivity,
@@ -195,8 +541,6 @@
     squared_estimate_final_matrix,
 ):
     levels_all = entry_layer_matrix.shape[0]
-    w_in_bf = entry_layer_matrix.astype(jnp.bfloat16)
-    w_out_bf = final_layer_matrix.astype(jnp.bfloat16)
     total_cols = (
         seed_sensitivity.shape[1]
         * seed_sensitivity.shape[2]
@@ -204,35 +548,6 @@
         * lax.axis_size("sec")
     )
     factor = 1.0 / math.sqrt(total_cols)
-    costate = transport(
-        seed_sensitivity, zonal_flow_ratio, meridional_flow_ratio, updraft_flow_ratio
-    )
-    costate_bf = costate.astype(jnp.bfloat16)
-    profiles, back_cols = (
-        lax.all_to_all(thermal_departure, "lev", split_axis=1, concat_axis=0, tiled=True),
-        lax.all_to_all(costate_bf, "lev", split_axis=1, concat_axis=0, tiled=True),
-    )
-    flat = profiles.reshape(levels_all, -1)
-    pre = lax.dot_general(
-        w_in_bf, flat, (((0,), (0,)), ((), ())), preferred_element_type=jnp.float32
-    )
-    act = jnp.tanh(pre)
-    col_shape = back_cols.shape
-    back = back_cols.reshape(levels_all, -1)
-    act_bf = act.astype(jnp.bfloat16)
-    part_out = lax.dot_general(
-        act_bf, back, (((1,), (1,)), ((), ())), preferred_element_type=jnp.float32
-    )
-    d_act = jnp.dot(w_out_bf, back, preferred_element_type=jnp.float32)
-    d_pre = (d_act * (1.0 - act * act)).astype(jnp.bfloat16)
-    part_in = lax.dot_general(
-        flat, d_pre, (((1,), (1,)), ((), ())), preferred_element_type=jnp.float32
-    )
-    d_input = jnp.dot(w_in_bf, d_pre, preferred_element_type=jnp.float32).astype(jnp.bfloat16)
-    d_levels = lax.all_to_all(
-        d_input.reshape(col_shape), "lev", split_axis=0, concat_axis=1, tiled=True
-    )
-    input_cotangent = costate + d_levels.astype(jnp.float32)
     sizes = tuple(lax.axis_size(axis) for axis in REDUCED)
     levs = sizes[2]
 
@@ -246,8 +561,13 @@
             unslots(value[:, :half], levs, levels_all),
         )
 
+    weight = packed(final_layer_matrix, entry_layer_matrix)
+    input_cotangent, grad = columns_back(
+        sizes, thermal_departure, seed_sensitivity, zonal_flow_ratio, meridional_flow_ratio,
+        updraft_flow_ratio, weight,
+    )
     new_weight, new_first, new_second = reduce_update(
-        sizes, factor, packed(part_out, part_in), packed(final_layer_matrix, entry_layer_matrix),
+        sizes, factor, grad, weight,
         packed(mean_estimate_final_matrix, mean_estimate_entry_matrix),
         packed(squared_estimate_final_matrix, squared_estimate_entry_matrix),
     )

time: 153 us -> 81 us (0.53)
  Pallas kernels: 18.7 us -> 64.5 us
  local copies, waits for them, and re-layouts: 57.3 us -> 13.2 us
  other arithmetic: 31.5 us -> 2.21 us
  starting transfers between devices: 20.1 us -> 0 us
  matrix products: 12.9 us -> 0 us
  blocking collectives: 10.6 us -> 0 us
    pallas_call x0 -> x1, Pallas kernels: none -> 49.1 us  [columns_back(): pl.pallas_call(functools.partial(column_kernel, sizes), out_shape=[jax.Sh...]
    slice x28 -> x0, local copies, waits for them, and re-layouts: 27.8 us -> none  [the longest x4 7.52 us: adjoint_step(): next_y = jnp.concatenate([costate[:, :, 1:], edge_y], axis=2)]
    add x4 -> x0, other arithmetic: 21.7 us -> none  [the longest x3 20.1 us: adjoint_step(): costate + zonal_flow_ratio * (next_x - costate)]
    ppermute x12 -> x0, starting transfers between devices: 16.6 us -> none  [the longest x8 10.5 us: from_behind(): lax.ppermute(value, axis, [(source, source + steps) for source in range(f...]
    dot_general x5 -> x0, matrix products: 12.9 us -> none  [the longest x1 4.69 us: shards(): lax.dot_general(w_in_bf, flat, (((0,), (0,)), ((), ())), preferred_elemen...]
    all_to_all x2 -> x0, blocking collectives: 10.6 us -> none  [the longest x1 5.42 us: shards(): lax.all_to_all(costate_bf, 'lev', split_axis=1, concat_axis=0, tiled=True)]
    convert_element_type x2 -> x0, other arithmetic: 7 us -> none  [the longest x1 6.76 us: shards(): costate_bf = costate.astype(jnp.bfloat16)]
    ppermute x4 -> x0, local copies, waits for them, and re-layouts: 5.31 us -> none  [from_behind(): lax.ppermute(value, axis, [(source, source + steps) for source in range(f...]
  transfers between devices with their start and end apart: 13 -> 0, of which waited for: 0 -> 0; matrix products, arithmetic and copies ran while one was open for 35% -> 0% of each run, Pallas kernels for 12% -> 0%
where the time goes in v2:
time: 81 us; the launch traced here: 80.7 us
  Pallas kernels  64.5 us (80%)
  local copies, waits for them, and re-layouts  13.2 us (16%)
  other arithmetic  2.21 us (3%)
    pallas_call x1, Pallas kernels, columns_back(): pl.pallas_call(functools.partial(column_kernel, sizes), out_shape=[jax.Sh...  49.1 us
    pallas_call x1, Pallas kernels, reduce_update(): pl.pallas_call(functools.partial(reduce_kernel, sizes, factor), out_shape...  15.4 us
    reshape x6, local copies, waits for them, and re-layouts, unslots(): return value.reshape(value.shape[0], levels_all)  3.99 us
    unnamed x17, local copies, waits for them, and re-layouts  3.64 us
    concatenate x4, other arithmetic, packed(): return jnp.concatenate([slots(of_out, levs), slots(of_in.T, levs)], axis=1)  2.21 us
    reshape x6, local copies, waits for them, and re-layouts, slots(): value = value.reshape(value.shape[0], parts, levels)  2.1 us
    slice x2, local copies, waits for them, and re-layouts, unpacked(): value[:, :half]  1.92 us

profile of v2, /device:TPU:0, one launch (start us, length us, event | category | flops | bytes accessed | tf_op | source)
XLA Modules:
  0.0 80.7 jit_solution(778772539540363520)
XLA Ops:
  0.6 0.9 %reshape.97 = f32[256,2,30]{0,2,1:T(8,128)S(1)} reshape(f32[256,60]{0,1:T(8,128)} %param.17) | data formatting | bytes 122880 | tf_op jit(solution)/shard_map/reshape | solution.py:35
  1.6 0.1 copy.22
  1.7 0.9 %reshape.99 = f32[256,2,30]{0,2,1:T(8,128)S(1)} reshape(f32[256,60]{0,1:T(8,128)} %bitcast.36) | data formatting | bytes 122880 | tf_op jit(solution)/shard_map/reshape | solution.py:35
  2.6 0.1 pad_maximum_fusion.weight_ref
  2.8 1.5 %copy-done = f32[30,64,256]{2,1,0:T(8,128)S(1)} copy-done((f32[30,64,256]{2,1,0:T(8,128)S(1)}, f32[30,64,256]{2,1,0:T(8,128)}, u32[]{:S(2)}) %copy-start) | copy-done | bytes 1966104
  4.3 49.1 %columns_back.1 = (f32[30,64,256]{2,1,0:T(8,128)S(1)}, f32[256,128]{1,0:T(8,128)S(1)}) custom-call(bf16[30,64,256]{2,1,0:T(8,128)(2,1)S(1)} %copy-done.1, f32[30,64,256]{2,1,0:T(8,128)S(1)} %copy-done, f32[30,64,256]{2,1,0:T(8,128)} %zonal_hbm.1, f32[30,64,256]{2,1,0:T(8,128)} %merid_hbm.1, f32[30,64,256]{2,1,0:T(8,128)} %updraft_hbm.1, ...), custom_call_target="tpu_custom_call" | custom-call | tf_op jit(solution)/shard_map/columns_back/pallas_call | solution.py:500
  53.4 0.6 copy-done.2
  54.1 0.1 copy.24
  54.2 0.2 concatenate.17
  54.4 0.1 copy.25
  54.6 0.2 concatenate.18
  54.8 0.8 pad_maximum_fusion.1.weight_ref
  55.9 0.7 pad_maximum_fusion.2.first_ref
  56.9 0.7 pad_maximum_fusion.3.second_ref
  57.6 15.4 %reduce_update.1 = (f32[16,16,128]{2,1,0:T(8,128)}, f32[16,128]{1,0:T(8,128)}, f32[16,128]{1,0:T(8,128)}) custom-call(f32[16,16,128]{2,1,0:T(8,128)} %bitcast.26, f32[16,16,128]{2,1,0:T(8,128)} %pad_maximum_fusion.1.weight_ref, f32[16,128]{1,0:T(8,128)} %pad_maximum_fusion.2.first_ref, f32[16,128]{1,0:T(8,128)} %pad_maximum_fusion.3.second_ref), custom_call_target="tpu_custom_call" | custom-call | tf_op jit(solution)/shard_map/reduce_update/pallas_call | solution.py:130
  73.0 0.8 %fusion.1 = (f32[16,64]{1,0:T(8,128)S(1)}, f32[16,64]{1,0:T(8,128)S(1)}, f32[16,64]{1,0:T(8,128)S(1)}, f32[16,64]{1,0:T(8,128)S(1)}) fusion(f32[16,128]{1,0:T(8,128)} %get-tuple-element.16, f32[16,128]{1,0:T(8,128)} %get-tuple-element.15), kind=kLoop, calls=%fused_computation.5 | loop fusion | bytes 32768 | tf_op jit(solution)/shard_map/slice | solution.py:561
  74.0 0.7 reshape.116
  74.7 0.7 reshape.118
  75.5 0.7 reshape.120
  76.2 0.7 reshape.122
  76.9 1.1 %fusion = (f32[256,64]{1,0:T(8,128)S(1)}, f32[256,64]{1,0:T(8,128)S(1)}) fusion(f32[256,128]{1,0:T(8,128)} %bitcast.29), kind=kLoop, calls=%fused_computation.4 | loop fusion | bytes 262144 | tf_op jit(solution)/shard_map/slice | solution.py:561
  78.1 0.6 reshape.112
  78.8 0.6 reshape.114
  79.4 1.3 %copy.31 = f32[30,64,256]{2,1,0:T(8,128)} copy(f32[30,64,256]{2,1,0:T(8,128)S(1)} %get-tuple-element.32) | data formatting | bytes 3932160
  (33 shorter events, 1.3 us)
Async XLA Ops:
  0.6 2.1 %copy-start.1 = (bf16[30,64,256]{2,1,0:T(8,128)(2,1)S(1)}, bf16[30,64,256]{2,1,0:T(8,128)(2,1)}, u32[]{:S(2)}) copy-start(bf16[30,64,256]{2,1,0:T(8,128)(2,1)} %theta_hbm.1) | copy-start | bytes 2949124
  2.8 1.5 %copy-start = (f32[30,64,256]{2,1,0:T(8,128)S(1)}, f32[30,64,256]{2,1,0:T(8,128)}, u32[]{:S(2)}) copy-start(f32[30,64,256]{2,1,0:T(8,128)} %seed_hbm.1) | copy-start | bytes 5898244
  4.3 51.2 %copy-start.3 = (f32[16,60]{1,0:T(8,128)S(1)}, f32[16,60]{1,0:T(8,128)}, u32[]{:S(2)}) copy-start(f32[16,60]{1,0:T(8,128)} %param.20) | copy-start | bytes 11524
  4.3 51.4 %copy-start.4 = (f32[60,16]{0,1:T(8,128)S(1)}, f32[60,16]{0,1:T(8,128)}, u32[]{:S(2)}) copy-start(f32[60,16]{0,1:T(8,128)} %param.18) | copy-start | bytes 11524
  53.4 0.7 copy-start.2
  54.1 2.5 %copy-start.5 = (f32[16,60]{1,0:T(8,128)S(1)}, f32[16,60]{1,0:T(8,128)}, u32[]{:S(2)}) copy-start(f32[16,60]{1,0:T(8,128)} %param.21) | copy-start | bytes 11524
  54.1 2.6 %copy-start.6 = (f32[60,16]{0,1:T(8,128)S(1)}, f32[60,16]{0,1:T(8,128)}, u32[]{:S(2)}) copy-start(f32[60,16]{0,1:T(8,128)} %param.19) | copy-start | bytes 11524

commit v3 on v2

--- a/solution.py
+++ b/solution.py
@@ -9,6 +9,7 @@
 from jax.sharding import PartitionSpec as P
 
 STEPS = 4
+GROUP = 4
 
 
 bias_first = 1.0 - 0.9**10
@@ -28,19 +29,6 @@
 
 def slot_size(levels):
     return -(-levels // 8) * 8
-
-
-def slots(value, parts):
-    levels = value.shape[1] // parts
-    value = value.reshape(value.shape[0], parts, levels)
-    value = jnp.pad(value, ((0, 0), (0, 0), (0, slot_size(levels) - levels)))
-    return value.reshape(value.shape[0], -1)
-
-
-def unslots(value, parts, levels_all):
-    slot = value.shape[1] // parts
-    value = value.reshape(value.shape[0], parts, slot)[:, :, : levels_all // parts]
-    return value.reshape(value.shape[0], levels_all)
 
 
 def peer_at(position, sizes):
@@ -57,10 +45,9 @@
     return (lax.axis_index("col") * secs + lax.axis_index("sec")) * levs + lax.axis_index("lev")
 
 
-def reduce_kernel(
-    sizes, factor, grad_ref, weight_ref, first_ref, second_ref,
-    new_weight_ref, new_first_ref, new_second_ref,
-    landed, piece, send_sems, recv_sems, out_sems, in_sems,
+def exchange(
+    sizes, factor, grad_ref, own_share, gathered, landed, piece,
+    send_sems, recv_sems, out_sems, in_sems,
 ):
     count = sizes[0] * sizes[1] * sizes[2]
     me = own_position(sizes)
@@ -85,7 +72,7 @@
     def spread(hop):
         peer = lax.rem(me + hop, count)
         return pltpu.make_async_remote_copy(
-            src_ref=piece, dst_ref=new_weight_ref.at[me],
+            src_ref=piece, dst_ref=gathered.at[me],
             send_sem=out_sems.at[hop], recv_sem=in_sems.at[hop],
             device_id=peer_at(peer, sizes), device_id_type=MESH,
         )
@@ -97,54 +84,128 @@
         lax.fori_loop(1, count, body, 0)
 
     start(share)
+    weight, first, second = own_share(me)
 
     def add(hop, total):
         share(hop).wait_recv()
         return total + landed[hop]
 
     total = lax.fori_loop(1, count, add, grad_ref[me])
-    piece[...], new_first_ref[...], new_second_ref[...] = adam_update(
-        weight_ref[me], total * factor, first_ref[...], second_ref[...]
-    )
+    new, new_first, new_second = adam_update(weight, total * factor, first, second)
+    piece[...] = new
     start(spread)
-    new_weight_ref[me] = piece[...]
+    gathered[me] = new
+
+    def leave(hop, carry):
+        share(hop).wait_send()
+        return carry
 
     def arrive(hop, carry):
         spread(hop).wait_recv()
-        return carry
-
-    def leave(hop, carry):
-        share(hop).wait_send()
         spread(hop).wait_send()
         return carry
 
-    lax.fori_loop(1, count, arrive, 0)
     lax.fori_loop(1, count, leave, 0)
-
-
-def reduce_update(sizes, factor, grad, weight, first, second):
+    return new_first, new_second, lambda: lax.fori_loop(1, count, arrive, 0)
+
+
+def reduce_kernel(
+    sizes, factor, grad_ref, w_in_ref, w_out_ref, first_in, second_in, first_out, second_out,
+    new_w_in, new_w_out, new_first_in, new_second_in, new_first_out, new_second_out,
+    gathered, landed, piece, wide, tall, few, turned, *sems,
+):
+    levels, hidden = w_in_ref.shape
+    rows, lanes = piece.shape
+    middle = lanes // 2
+
+    def packed(of_in, of_out):
+        few[...] = jnp.zeros_like(few)
+        few[:, :levels] = of_out[...]
+        turned[...] = jnp.zeros_like(turned)
+        turned[middle : middle + levels, :rows] = of_in[...]
+        return few[...] + turned[...].T[:rows]
+
+    def own_share(me):
+        tall[...] = jnp.zeros_like(tall)
+        tall[middle : middle + levels] = w_in_ref[...]
+        wide[...] = jnp.zeros_like(wide)
+        wide[:, :levels] = w_out_ref[...]
+        wide[...] = wide[...] + tall[...].T
+        weight = wide[pl.ds(pl.multiple_of(me * rows, rows), rows), :]
+        return weight, packed(first_in, first_out), packed(second_in, second_out)
+
+    def unpack(value, of_in, of_out):
+        of_out[...] = value[:, :levels]
+        turned[:rows] = value
+        of_in[...] = turned[...].T[middle : middle + levels, :rows]
+
+    new_first, new_second, arrive = exchange(
+        sizes, factor, grad_ref, own_share, gathered, landed, piece, *sems
+    )
+    unpack(new_first, new_first_in, new_first_out)
+    unpack(new_second, new_second_in, new_second_out)
+    arrive()
+    weights = gathered[...].reshape(hidden, lanes)
+    new_w_out[...] = weights[:, :levels]
+    new_w_in[...] = weights.T[middle : middle + levels]
+
+
+def narrow_kernel(
+    sizes, factor, grad_ref, weight_ref, first_ref, second_ref,
+    gathered, new_first_ref, new_second_ref, landed, piece, *sems,
+):
+    new_first_ref[...], new_second_ref[...], arrive = exchange(
+        sizes, factor, grad_ref, lambda me: (weight_ref[me], first_ref[...], second_ref[...]),
+        gathered, landed, piece, *sems,
+    )
+    arrive()
+
+
+def reduce_update(sizes, factor, grad, w_in, w_out, first_in, second_in, first_out, second_out):
     count = sizes[0] * sizes[1] * sizes[2]
-    rows, lanes = first.shape
+    levels, hidden = w_in.shape
+    lanes = grad.shape[1]
+    rows, middle = hidden // count, lanes // 2
+    f32 = jnp.float32
     vmem = pl.BlockSpec(memory_space=pltpu.VMEM)
-    dma = pltpu.SemaphoreType.DMA((count,))
-    new_weight, new_first, new_second = pl.pallas_call(
-        functools.partial(reduce_kernel, sizes, factor),
-        out_shape=[
-            jax.ShapeDtypeStruct((count, rows, lanes), jnp.float32),
-            jax.ShapeDtypeStruct((rows, lanes), jnp.float32),
-            jax.ShapeDtypeStruct((rows, lanes), jnp.float32),
-        ],
-        in_specs=[vmem] * 4,
-        out_specs=[vmem] * 3,
-        scratch_shapes=[
-            pltpu.VMEM((count, rows, lanes), jnp.float32),
-            pltpu.VMEM((rows, lanes), jnp.float32),
-            dma, dma, dma, dma,
-        ],
-        compiler_params=pltpu.CompilerParams(collective_id=1, has_side_effects=True),
-        name="reduce_update",
-    )(grad.reshape(count, rows, lanes), weight.reshape(count, rows, lanes), first, second)
-    return new_weight.reshape(count * rows, lanes), new_first, new_second
+    shares = (count, rows, lanes)
+    sems = [pltpu.SemaphoreType.DMA((count,))] * 4
+    grad = grad.reshape(shares)
+
+    def call(kernel, shapes, scratch, args):
+        return pl.pallas_call(
+            functools.partial(kernel, sizes, factor),
+            out_shape=[jax.ShapeDtypeStruct(shape, f32) for shape in shapes],
+            in_specs=[vmem] * len(args),
+            out_specs=[vmem] * len(shapes),
+            scratch_shapes=[pltpu.VMEM(shape, f32) for shape in scratch] + sems,
+            compiler_params=pltpu.CompilerParams(collective_id=1, has_side_effects=True),
+            name="reduce_update",
+        )(*args)
+
+    if rows % 8 == 0 and rows <= lanes:
+        return call(
+            reduce_kernel,
+            [w_in.shape, w_out.shape, (levels, rows), (levels, rows), (rows, levels), (rows, levels)],
+            [shares, shares, (rows, lanes), (hidden, lanes), (lanes, hidden), (rows, lanes),
+             (lanes, lanes)],
+            (grad, w_in, w_out, first_in, second_in, first_out, second_out),
+        )
+
+    def packed(of_in, of_out):
+        pad = ((0, 0), (0, middle - levels))
+        return jnp.concatenate([jnp.pad(of_out, pad), jnp.pad(of_in.T, pad)], axis=1)
+
+    def unpacked(value):
+        return value[:, middle : middle + levels].T, value[:, :levels]
+
+    weight, first, second = call(
+        narrow_kernel, [shares, (rows, lanes), (rows, lanes)], [shares, (rows, lanes)],
+        (grad, packed(w_in, w_out).reshape(shares), packed(first_in, first_out),
+         packed(second_in, second_out)),
+    )
+    of_in, of_out = zip(*map(unpacked, (weight.reshape(hidden, lanes), first, second)))
+    return of_in[0], of_out[0], of_in[1], of_in[2], of_out[1], of_out[2]
 
 
 def halves(levels):
@@ -153,10 +214,10 @@
 
 
 def column_kernel(
-    sizes, theta_hbm, seed_hbm, zonal_hbm, merid_hbm, updraft_hbm, weight_ref,
+    sizes, theta_hbm, seed_hbm, zonal_hbm, merid_hbm, updraft_hbm, w_in_ref, w_out_ref,
     out_hbm, grad_ref,
     v, zonal, merid, updraft, edge_x, halo_x, edge_y, halo_y, edge_z, halo_z,
-    theta_own, theta_far, profile, back_far, d_in, d_far, w_out, w_in, w_in_t,
+    theta_own, theta_far, profile, back_far, d_in, d_far, w_out, w_in, w_in_t, wide, tall,
     load_sems, seed_sems, theta_sems, x_sems, y_sems, z_sems, back_sems, d_sems, out_sems,
 ):
     cols, secs, _ = sizes
@@ -271,7 +332,7 @@
 
     tiles = rows // 8
     lane = lax.broadcasted_iota(jnp.int32, (8, 128), 1)
-    last_lane = lax.broadcasted_iota(jnp.int32, (rows, lanes), 1) == lanes - 1
+    last_lane = lax.broadcasted_iota(jnp.int32, (rows, 128), 1) == 127
     last_row = lax.broadcasted_iota(jnp.int32, (rows, lanes), 0) == rows - 1
 
     def keep_edges(value, z, low, step, packed):
@@ -297,17 +358,33 @@
             def _():
                 z_copy(step).start()
 
-    def advance(z, low, step, part, above):
-        now = whole(v, z)
-        strip = pltpu.roll(halo_y[step, part], lax.rem(128 - (z - low) * tiles, 128), axis=1)
-        column = jnp.concatenate([strip[:, tile : tile + 1] for tile in range(tiles)], axis=0)
-        next_x = jnp.where(last_row, halo_x[step, pl.ds(z, 1), :], pltpu.roll(now, rows - 1, axis=0))
-        next_y = jnp.where(last_lane, column, pltpu.roll(now, lanes - 1, axis=1))
-        new = (
-            now + zonal[z] * (next_x - now) + merid[z] * (next_y - now) + updraft[z] * (above - now)
-        )
-        lay(v, z, new)
-        return new
+    def advance(first, count, low, step, part, packed, above=None):
+        levels_now = [whole(v, first + at) for at in range(count)]
+        levels_now.append(whole(v, first + count) if above is None else above)
+        strip = halo_y[step, part]
+        news = []
+        for at in range(count):
+            z, now, over = first + at, levels_now[at], levels_now[at + 1]
+            side = jnp.concatenate([
+                pltpu.roll(strip, lax.rem(255 - (z - low) * tiles - tile, 128), axis=1)
+                for tile in range(tiles)
+            ], axis=0)
+            next_x = jnp.where(
+                last_row, halo_x[step, pl.ds(z, 1), :], pltpu.roll(now, rows - 1, axis=0)
+            )
+            shifted = pltpu.roll(now, lanes - 1, axis=1)
+            next_y = jnp.concatenate([
+                shifted[:, : lanes - 128], jnp.where(last_lane, side, shifted[:, lanes - 128 :])
+            ], axis=1)
+            news.append(
+                now + zonal[z] * (next_x - now) + merid[z] * (next_y - now)
+                + updraft[z] * (over - now)
+            )
+        for at, new in enumerate(news):
+            lay(v, first + at, new)
+            if step + 1 < STEPS:
+                packed = keep_edges(new, first + at, low, step + 1, packed)
+        return packed
 
     nothing = jnp.zeros((8, 128), jnp.float32)
     for part, (low, high) in enumerate(parts):
@@ -318,11 +395,16 @@
         )
         send_edges(0, part, packed)
 
-    weights = weight_ref[...]
-    middle = weights.shape[1] // 2
-    w_out[...] = weights[:, :middle].astype(jnp.bfloat16)
-    w_in[...] = weights[:, middle:].astype(jnp.bfloat16)
-    w_in_t[...] = weights[:, middle:].T.astype(jnp.bfloat16)
+    wide[...] = jnp.zeros_like(wide)
+    wide[:, : 2 * levels] = w_out_ref[...]
+    across = lax.broadcasted_iota(jnp.int32, wide.shape, 1)
+    by_slot = jnp.where(across < levels, wide[...], pltpu.roll(wide[...], slot - levels, axis=1))
+    w_out[...] = by_slot[:, : 2 * slot].astype(jnp.bfloat16)
+    tall[...] = jnp.zeros_like(tall)
+    tall[0:levels] = w_in_ref[0:levels]
+    tall[slot : slot + levels] = w_in_ref[levels:]
+    w_in_t[...] = tall[...].astype(jnp.bfloat16)
+    w_in[...] = tall[...].T.astype(jnp.bfloat16)
     v[:, levels:] = jnp.zeros((pieces, slot - levels, rows, 128), jnp.float32)
     back_far[:, levels:] = jnp.zeros((pieces, slot - levels, half, 128), jnp.float32)
     for start in (levels, slot + levels):
@@ -351,22 +433,23 @@
                 y_copy(step, part).wait_recv()
 
             more = step + 1 < STEPS
-            inner = high if part == 0 else high - 1
-
-            def body(z, packed):
-                new = advance(z, low, step, part, whole(v, z + 1))
-                return keep_edges(new, z, low, step + 1, packed) if more else packed
-
-            packed = lax.fori_loop(low, inner, body, nothing)
+            groups = (high - low - (GROUP if part else 0)) // GROUP
+            left = high - low - groups * GROUP
+
+            def body(at, packed):
+                return advance(low + at * GROUP, GROUP, low, step, part, packed)
+
+            packed = lax.fori_loop(0, groups, body, nothing)
             if part == 1:
 
                 @pl.when(lev == 0)
                 def _():
                     z_copy(step).wait_recv()
 
-                new = advance(inner, low, step, part, halo_z[step])
-                if more:
-                    packed = keep_edges(new, inner, low, step + 1, packed)
+            if left:
+                packed = advance(
+                    high - left, left, low, step, part, packed, halo_z[step] if part else None
+                )
             if more:
                 send_edges(step + 1, part, packed)
             else:
@@ -450,6 +533,13 @@
 
     chunks = half // chunk
     lax.fori_loop(0, chunks, network, 0)
+    slotted = grad_ref[...]
+    at_slot = lax.rem(lax.broadcasted_iota(jnp.int32, slotted.shape, 1), 2 * slot)
+    grad_ref[...] = jnp.where(
+        at_slot < levels, slotted,
+        pltpu.roll(slotted, slotted.shape[1] - (slot - levels), axis=1),
+    )
+
     def finish(at, carry):
         d_copy(at).wait_recv()
         span = pl.ds(pl.multiple_of(at * chunk, chunk), chunk)
@@ -488,9 +578,9 @@
             z_copy(step).wait_send()
 
 
-def columns_back(sizes, theta, seed, zonal, merid, updraft, weight):
+def columns_back(sizes, theta, seed, zonal, merid, updraft, weight_in, weight_out):
     levels, rows, lanes = seed.shape
-    hidden, width = weight.shape
+    hidden, width = weight_out.shape[0], 4 * slot_size(levels)
     slot, half, pieces = width // 4, rows // 2, lanes // 128
     f32, bf16 = jnp.float32, jnp.bfloat16
     hbm = pl.BlockSpec(memory_space=pl.ANY)
@@ -503,7 +593,7 @@
             jax.ShapeDtypeStruct((levels, rows, lanes), f32),
             jax.ShapeDtypeStruct((hidden, width), f32),
         ],
-        in_specs=[hbm] * 5 + [vmem],
+        in_specs=[hbm] * 5 + [vmem] * 2,
         out_specs=[hbm, vmem],
         scratch_shapes=[
             pltpu.VMEM((pieces, slot, rows, 128), f32), ratio, ratio, ratio,
@@ -517,6 +607,7 @@
             pltpu.VMEM((pieces, levels, half, 128), f32),
             pltpu.VMEM((hidden, width // 2), bf16), pltpu.VMEM((hidden, width // 2), bf16),
             pltpu.VMEM((width // 2, hidden), bf16),
+            pltpu.VMEM((hidden, width), f32), pltpu.VMEM((width // 2, hidden), f32),
             dma((3, 2)), dma((pieces, 2)), dma((3,)), dma((2, STEPS, 2)), dma((2, STEPS, 2)), dma((2, STEPS)),
             dma((2, 2)), dma((2, half // 8)), dma((2, half // 8)),
         ],
@@ -524,7 +615,7 @@
             collective_id=2, has_side_effects=True, vmem_limit_bytes=48 * 1024 * 1024
         ),
         name="columns_back",
-    )(theta, seed, zonal, merid, updraft, weight)
+    )(theta, seed, zonal, merid, updraft, weight_in, weight_out)
 
 
 def shards(
@@ -540,7 +631,6 @@
     mean_estimate_final_matrix,
     squared_estimate_final_matrix,
 ):
-    levels_all = entry_layer_matrix.shape[0]
     total_cols = (
         seed_sensitivity.shape[1]
         * seed_sensitivity.shape[2]
@@ -549,39 +639,14 @@
     )
     factor = 1.0 / math.sqrt(total_cols)
     sizes = tuple(lax.axis_size(axis) for axis in REDUCED)
-    levs = sizes[2]
-
-    def packed(of_out, of_in):
-        return jnp.concatenate([slots(of_out, levs), slots(of_in.T, levs)], axis=1)
-
-    def unpacked(value):
-        half = value.shape[1] // 2
-        return (
-            unslots(value[:, half:], levs, levels_all).T,
-            unslots(value[:, :half], levs, levels_all),
-        )
-
-    weight = packed(final_layer_matrix, entry_layer_matrix)
     input_cotangent, grad = columns_back(
         sizes, thermal_departure, seed_sensitivity, zonal_flow_ratio, meridional_flow_ratio,
-        updraft_flow_ratio, weight,
-    )
-    new_weight, new_first, new_second = reduce_update(
-        sizes, factor, grad, weight,
-        packed(mean_estimate_final_matrix, mean_estimate_entry_matrix),
-        packed(squared_estimate_final_matrix, squared_estimate_entry_matrix),
-    )
-    new_w_in, new_w_out = unpacked(new_weight)
-    new_first_in, new_first_out = unpacked(new_first)
-    new_second_in, new_second_out = unpacked(new_second)
-    return (
-        input_cotangent,
-        new_w_in,
-        new_w_out,
-        new_first_in,
-        new_second_in,
-        new_first_out,
-        new_second_out,
+        updraft_flow_ratio, entry_layer_matrix, final_layer_matrix,
+    )
+    return input_cotangent, *reduce_update(
+        sizes, factor, grad, entry_layer_matrix, final_layer_matrix,
+        mean_estimate_entry_matrix, squared_estimate_entry_matrix,
+        mean_estimate_final_matrix, squared_estimate_final_matrix,
     )
 
 

time: 81 us -> 65.7 us (0.81)
  Pallas kernels: 64.5 us -> 50.4 us
  other arithmetic: 2.21 us -> 0 us
  local copies, waits for them, and re-layouts: 13.2 us -> 14.2 us
    pallas_call x1, Pallas kernels: 49.1 us -> 36.2 us  [columns_back(): pl.pallas_call(functools.partial(column_kernel, sizes), out_shape=[jax.Sh...]
    unnamed x17 -> x30, local copies, waits for them, and re-layouts: 3.64 us -> 14.2 us
    reshape x22 -> x0, local copies, waits for them, and re-layouts: 6.92 us -> none  [the longest x6 3.99 us: unslots(): return value.reshape(value.shape[0], levels_all)]
    concatenate x4 -> x0, other arithmetic: 2.21 us -> none  [packed(): return jnp.concatenate([slots(of_out, levs), slots(of_in.T, levs)], axis=1)]
    slice x2 -> x0, local copies, waits for them, and re-layouts: 1.92 us -> none  [unpacked(): value[:, :half]]
    pallas_call x1, Pallas kernels: 15.4 us -> 14.2 us  [call(): pl.pallas_call(functools.partial(kernel, sizes, factor), out_shape=[jax.S...]
where the time goes in v3:
time: 65.7 us; the launch traced here: 65.2 us
  Pallas kernels  50.4 us (77%)
  local copies, waits for them, and re-layouts  14.2 us (22%)
  between operations  0.69 us (1%)
    pallas_call x1, Pallas kernels, columns_back(): pl.pallas_call(functools.partial(column_kernel, sizes), out_shape=[jax.Sh...  36.2 us
    unnamed x30, local copies, waits for them, and re-layouts  14.2 us
    pallas_call x1, Pallas kernels, call(): pl.pallas_call(functools.partial(kernel, sizes, factor), out_shape=[jax.S...  14.2 us

profile of v3, /device:TPU:0, one launch (start us, length us, event | category | flops | bytes accessed | tf_op | source)
XLA Modules:
  0.0 65.2 jit_solution(4144674208176550342)
XLA Ops:
  0.6 0.9 %copy.18.w_out_ref = f32[256,60]{1,0:T(8,128)S(1)} copy(f32[256,60]{0,1:T(8,128)} %param.17) | data formatting | bytes 122880 | tf_op args[6]
  1.6 0.0 copy-start
  1.6 1.5 %copy-done = f32[30,64,256]{2,1,0:T(8,128)S(1)} copy-done((f32[30,64,256]{2,1,0:T(8,128)S(1)}, f32[30,64,256]{2,1,0:T(8,128)}, u32[]{:S(2)}) %copy-start) | copy-done | bytes 1966104
  3.1 1.2 %copy-done.2 = bf16[30,64,256]{2,1,0:T(8,128)(2,1)S(1)} copy-done((bf16[30,64,256]{2,1,0:T(8,128)(2,1)S(1)}, bf16[30,64,256]{2,1,0:T(8,128)(2,1)}, u32[]{:S(2)}) %copy-start.2) | copy-done | bytes 983064
  4.3 0.8 %copy-done.3 = f32[60,256]{1,0:T(8,128)S(1)} copy-done((f32[60,256]{1,0:T(8,128)S(1)}, f32[60,256]{1,0:T(8,128)}, u32[]{:S(2)}) %copy-start.3) | copy-done | bytes 61464
  5.2 36.2 %columns_back.1 = (f32[30,64,256]{2,1,0:T(8,128)S(1)}, f32[256,128]{1,0:T(8,128)S(1)}) custom-call(bf16[30,64,256]{2,1,0:T(8,128)(2,1)S(1)} %copy-done.2, f32[30,64,256]{2,1,0:T(8,128)S(1)} %copy-done, f32[30,64,256]{2,1,0:T(8,128)} %zonal_hbm.1, f32[30,64,256]{2,1,0:T(8,128)} %merid_hbm.1, f32[30,64,256]{2,1,0:T(8,128)} %updraft_hbm.1, ...), custom_call_target="tpu_custom_call" | custom-call | tf_op jit(solution)/shard_map/columns_back/pallas_call | solution.py:590
  41.4 0.0 copy-done.1
  41.4 0.0 copy-start.4
  41.4 0.6 copy-done.4
  42.1 0.0 copy-done.6
  42.1 0.7 %copy.20.first_in = f32[60,16]{1,0:T(8,128)} copy(f32[60,16]{0,1:T(8,128)S(1)} %copy-done.6) | data formatting | bytes 7680 | tf_op args[7]
  42.8 0.0 copy-done.7
  42.8 0.7 %copy.21.second_in = f32[60,16]{1,0:T(8,128)} copy(f32[60,16]{0,1:T(8,128)S(1)} %copy-done.7) | data formatting | bytes 7680 | tf_op args[8]
  43.5 14.2 %reduce_update.1 = (f32[60,256]{1,0:T(8,128)}, f32[256,60]{1,0:T(8,128)}, f32[60,16]{1,0:T(8,128)}, f32[60,16]{1,0:T(8,128)}, f32[16,60]{1,0:T(8,128)}, /*index=5*/f32[16,60]{1,0:T(8,128)}) custom-call(f32[16,16,128]{2,1,0:T(8,128)} %bitcast.1, f32[60,256]{1,0:T(8,128)} %w_in_ref.3, f32[256,60]{1,0:T(8,128)} %copy-done.1, f32[60,16]{1,0:T(8,128)} %copy.20.first_in, ...), custom_call_target="tpu_custom_call" | custom-call | tf_op jit(solution)/shard_map/reduce_update/pallas_call | solution.py:176
  57.7 1.6 %copy.22 = f32[256,60]{0,1:T(8,128)} copy(f32[256,60]{1,0:T(8,128)} %get-tuple-element.25) | data formatting | bytes 122880
  59.3 1.4 %copy.23 = f32[60,16]{0,1:T(8,128)} copy(f32[60,16]{1,0:T(8,128)} %get-tuple-element.26) | data formatting | bytes 7680
  60.7 1.4 %copy.24 = f32[60,16]{0,1:T(8,128)} copy(f32[60,16]{1,0:T(8,128)} %get-tuple-element.27) | data formatting | bytes 7680
  62.1 1.3 %copy.29 = f32[30,64,256]{2,1,0:T(8,128)} copy(f32[30,64,256]{2,1,0:T(8,128)S(1)} %get-tuple-element.37) | data formatting | bytes 3932160
  63.4 0.0 copy-done.5
  63.4 0.6 copy.30
  64.0 0.0 copy-done.9
  64.0 0.6 copy.31
  64.6 0.0 copy-done.8
  64.6 0.6 copy.32
  (8 shorter events, 0.0 us)
Async XLA Ops:
  1.6 1.5 %copy-start = (f32[30,64,256]{2,1,0:T(8,128)S(1)}, f32[30,64,256]{2,1,0:T(8,128)}, u32[]{:S(2)}) copy-start(f32[30,64,256]{2,1,0:T(8,128)} %seed_hbm.1) | copy-start | bytes 5898244
  3.1 1.2 %copy-start.2 = (bf16[30,64,256]{2,1,0:T(8,128)(2,1)S(1)}, bf16[30,64,256]{2,1,0:T(8,128)(2,1)}, u32[]{:S(2)}) copy-start(bf16[30,64,256]{2,1,0:T(8,128)(2,1)} %theta_hbm.1) | copy-start | bytes 2949124
  4.3 0.8 %copy-start.3 = (f32[60,256]{1,0:T(8,128)S(1)}, f32[60,256]{1,0:T(8,128)}, u32[]{:S(2)}) copy-start(f32[60,256]{1,0:T(8,128)} %w_in_ref.3) | copy-start | bytes 184324
  5.2 36.2 %copy-start.1 = (f32[256,60]{1,0:T(8,128)}, f32[256,60]{1,0:T(8,128)S(1)}, u32[]{:S(2)}) copy-start(f32[256,60]{1,0:T(8,128)S(1)} %copy.18.w_out_ref) | copy-start | bytes 184324
  5.2 36.9 %copy-start.6 = (f32[60,16]{0,1:T(8,128)S(1)}, f32[60,16]{0,1:T(8,128)}, u32[]{:S(2)}) copy-start(f32[60,16]{0,1:T(8,128)} %param.18) | copy-start | bytes 11524
  5.2 37.6 %copy-start.7 = (f32[60,16]{0,1:T(8,128)S(1)}, f32[60,16]{0,1:T(8,128)}, u32[]{:S(2)}) copy-start(f32[60,16]{0,1:T(8,128)} %param.19) | copy-start | bytes 11524
  41.4 0.7 %copy-start.4 = (f32[256,128]{1,0:T(8,128)}, f32[256,128]{1,0:T(8,128)S(1)}, u32[]{:S(2)}) copy-start(f32[256,128]{1,0:T(8,128)S(1)} %get-tuple-element.16) | copy-start | bytes 393220
  62.1 1.3 %copy-start.5 = (f32[60,256]{1,0:T(8,128)S(1)}, f32[60,256]{1,0:T(8,128)}, u32[]{:S(2)}) copy-start(f32[60,256]{1,0:T(8,128)} %get-tuple-element.38) | copy-start | bytes 184324
  62.1 1.9 %copy-start.9 = (f32[16,60]{1,0:T(8,128)S(1)}, f32[16,60]{1,0:T(8,128)}, u32[]{:S(2)}) copy-start(f32[16,60]{1,0:T(8,128)} %get-tuple-element.42) | copy-start | bytes 11524
  62.1 2.5 %copy-start.8 = (f32[16,60]{1,0:T(8,128)S(1)}, f32[16,60]{1,0:T(8,128)}, u32[]{:S(2)}) copy-start(f32[16,60]{1,0:T(8,128)} %get-tuple-element.43) | copy-start | bytes 11524

commit v4 on v3

--- a/solution.py
+++ b/solution.py
@@ -112,7 +112,7 @@
 def reduce_kernel(
     sizes, factor, grad_ref, w_in_ref, w_out_ref, first_in, second_in, first_out, second_out,
     new_w_in, new_w_out, new_first_in, new_second_in, new_first_out, new_second_out,
-    gathered, landed, piece, wide, tall, few, turned, *sems,
+    gathered, landed, piece, wide, tall, few, *sems,
 ):
     levels, hidden = w_in_ref.shape
     rows, lanes = piece.shape
@@ -121,23 +121,20 @@
     def packed(of_in, of_out):
         few[...] = jnp.zeros_like(few)
         few[:, :levels] = of_out[...]
-        turned[...] = jnp.zeros_like(turned)
-        turned[middle : middle + levels, :rows] = of_in[...]
-        return few[...] + turned[...].T[:rows]
+        few[:, middle : middle + levels] = of_in[...]
+        return few[...]
 
     def own_share(me):
         tall[...] = jnp.zeros_like(tall)
         tall[middle : middle + levels] = w_in_ref[...]
-        wide[...] = jnp.zeros_like(wide)
-        wide[:, :levels] = w_out_ref[...]
-        wide[...] = wide[...] + tall[...].T
+        tall[:levels] = w_out_ref[...]
+        wide[...] = tall[...].T
         weight = wide[pl.ds(pl.multiple_of(me * rows, rows), rows), :]
         return weight, packed(first_in, first_out), packed(second_in, second_out)
 
     def unpack(value, of_in, of_out):
         of_out[...] = value[:, :levels]
-        turned[:rows] = value
-        of_in[...] = turned[...].T[middle : middle + levels, :rows]
+        of_in[...] = value[:, middle : middle + levels]
 
     new_first, new_second, arrive = exchange(
         sizes, factor, grad_ref, own_share, gathered, landed, piece, *sems
@@ -146,8 +143,9 @@
     unpack(new_second, new_second_in, new_second_out)
     arrive()
     weights = gathered[...].reshape(hidden, lanes)
-    new_w_out[...] = weights[:, :levels]
-    new_w_in[...] = weights.T[middle : middle + levels]
+    turned = weights.T
+    new_w_out[...] = turned[:levels]
+    new_w_in[...] = turned[middle : middle + levels]
 
 
 def narrow_kernel(
@@ -183,14 +181,14 @@
             name="reduce_update",
         )(*args)
 
-    if rows % 8 == 0 and rows <= lanes:
-        return call(
+    if rows % 8 == 0:
+        w_in, w_out, m_in, v_in, m_out, v_out = call(
             reduce_kernel,
-            [w_in.shape, w_out.shape, (levels, rows), (levels, rows), (rows, levels), (rows, levels)],
-            [shares, shares, (rows, lanes), (hidden, lanes), (lanes, hidden), (rows, lanes),
-             (lanes, lanes)],
-            (grad, w_in, w_out, first_in, second_in, first_out, second_out),
-        )
+            [w_in.shape] * 2 + [(rows, levels)] * 4,
+            [shares, shares, (rows, lanes), (hidden, lanes), (lanes, hidden), (rows, lanes)],
+            (grad, w_in, w_out.T, first_in.T, second_in.T, first_out, second_out),
+        )
+        return w_in, w_out.T, m_in.T, v_in.T, m_out, v_out
 
     def packed(of_in, of_out):
         pad = ((0, 0), (0, middle - levels))
@@ -396,7 +394,9 @@
         send_edges(0, part, packed)
 
     wide[...] = jnp.zeros_like(wide)
-    wide[:, : 2 * levels] = w_out_ref[...]
+    tall[...] = jnp.zeros_like(tall)
+    tall[: 2 * levels] = w_out_ref[...]
+    wide[:, : 2 * slot] = tall[...].T
     across = lax.broadcasted_iota(jnp.int32, wide.shape, 1)
     by_slot = jnp.where(across < levels, wide[...], pltpu.roll(wide[...], slot - levels, axis=1))
     w_out[...] = by_slot[:, : 2 * slot].astype(jnp.bfloat16)
@@ -580,7 +580,7 @@
 
 def columns_back(sizes, theta, seed, zonal, merid, updraft, weight_in, weight_out):
     levels, rows, lanes = seed.shape
-    hidden, width = weight_out.shape[0], 4 * slot_size(levels)
+    hidden, width = weight_out.shape[1], 4 * slot_size(levels)
     slot, half, pieces = width // 4, rows // 2, lanes // 128
     f32, bf16 = jnp.float32, jnp.bfloat16
     hbm = pl.BlockSpec(memory_space=pl.ANY)
@@ -593,7 +593,7 @@
             jax.ShapeDtypeStruct((levels, rows, lanes), f32),
             jax.ShapeDtypeStruct((hidden, width), f32),
         ],
-        in_specs=[hbm] * 5 + [vmem] * 2,
+        in_specs=[pl.BlockSpec(memory_space=pltpu.HBM)] * 5 + [vmem] * 2,
         out_specs=[hbm, vmem],
         scratch_shapes=[
             pltpu.VMEM((pieces, slot, rows, 128), f32), ratio, ratio, ratio,
@@ -641,7 +641,7 @@
     sizes = tuple(lax.axis_size(axis) for axis in REDUCED)
     input_cotangent, grad = columns_back(
         sizes, thermal_departure, seed_sensitivity, zonal_flow_ratio, meridional_flow_ratio,
-        updraft_flow_ratio, entry_layer_matrix, final_layer_matrix,
+        updraft_flow_ratio, entry_layer_matrix, final_layer_matrix.T,
     )
     return input_cotangent, *reduce_update(
         sizes, factor, grad, entry_layer_matrix, final_layer_matrix,

time: 65.7 us -> 61.4 us (0.935)
  local copies, waits for them, and re-layouts: 14.2 us -> 10 us
    unnamed x30 -> x29, local copies, waits for them, and re-layouts: 14.2 us -> 10 us
where the time goes in v4:
time: 61.4 us; the launch traced here: 61.1 us
  Pallas kernels  50.4 us (82%)
  local copies, waits for them, and re-layouts  10 us (16%)
  between operations  0.72 us (1%)
    pallas_call x1, Pallas kernels, columns_back(): pl.pallas_call(functools.partial(column_kernel, sizes), out_shape=[jax.Sh...  36.2 us
    pallas_call x1, Pallas kernels, call(): pl.pallas_call(functools.partial(kernel, sizes, factor), out_shape=[jax.S...  14.1 us
    unnamed x29, local copies, waits for them, and re-layouts  10 us

profile of v4, /device:TPU:0, one launch (start us, length us, event | category | flops | bytes accessed | tf_op | source)
XLA Modules:
  0.0 61.1 jit_solution(8070416292815697666)
XLA Ops:
  0.6 0.0 copy-start
  0.6 1.5 %copy-done = f32[30,64,256]{2,1,0:T(8,128)S(1)} copy-done((f32[30,64,256]{2,1,0:T(8,128)S(1)}, f32[30,64,256]{2,1,0:T(8,128)}, u32[]{:S(2)}) %copy-start) | copy-done | bytes 1966104
  2.2 1.2 %copy-done.1 = bf16[30,64,256]{2,1,0:T(8,128)(2,1)S(1)} copy-done((bf16[30,64,256]{2,1,0:T(8,128)(2,1)S(1)}, bf16[30,64,256]{2,1,0:T(8,128)(2,1)}, u32[]{:S(2)}) %copy-start.1) | copy-done | bytes 983064
  3.4 0.8 %copy-done.2 = f32[60,256]{1,0:T(8,128)S(1)} copy-done((f32[60,256]{1,0:T(8,128)S(1)}, f32[60,256]{1,0:T(8,128)}, u32[]{:S(2)}) %copy-start.2) | copy-done | bytes 61464
  4.2 0.8 %copy-done.3 = f32[256,60]{0,1:T(8,128)S(1)} copy-done((f32[256,60]{0,1:T(8,128)S(1)}, f32[256,60]{0,1:T(8,128)}, u32[]{:S(2)}) %copy-start.3) | copy-done | bytes 61464
  5.1 36.2 %columns_back.1 = (f32[30,64,256]{2,1,0:T(8,128)S(1)}, f32[256,128]{1,0:T(8,128)S(1)}) custom-call(bf16[30,64,256]{2,1,0:T(8,128)(2,1)S(1)} %copy-done.1, f32[30,64,256]{2,1,0:T(8,128)S(1)} %copy-done, f32[30,64,256]{2,1,0:T(8,128)} %zonal_hbm.1, f32[30,64,256]{2,1,0:T(8,128)} %merid_hbm.1, f32[30,64,256]{2,1,0:T(8,128)} %updraft_hbm.1, ...), custom_call_target="tpu_custom_call" | custom-call | tf_op jit(solution)/shard_map/columns_back/pallas_call | solution.py:590
  41.3 0.0 copy-start.4
  41.3 0.6 %copy-done.4 = f32[256,128]{1,0:T(8,128)} copy-done((f32[256,128]{1,0:T(8,128)}, f32[256,128]{1,0:T(8,128)S(1)}, u32[]{:S(2)}) %copy-start.4) | copy-done | bytes 131096
  42.0 14.1 %reduce_update.1 = (f32[60,256]{1,0:T(8,128)}, f32[60,256]{1,0:T(8,128)}, f32[16,60]{1,0:T(8,128)}, f32[16,60]{1,0:T(8,128)}, f32[16,60]{1,0:T(8,128)}, /*index=5*/f32[16,60]{1,0:T(8,128)}) custom-call(f32[16,16,128]{2,1,0:T(8,128)} %bitcast.9, f32[60,256]{1,0:T(8,128)} %w_in_ref.3, f32[60,256]{1,0:T(8,128)} %bitcast.7, f32[16,60]{1,0:T(8,128)} %bitcast.11, ...), custom_call_target="tpu_custom_call" | custom-call | tf_op jit(solution)/shard_map/reduce_update/pallas_call | solution.py:174
  56.1 0.0 copy-start.6
  56.1 0.0 copy-start.5
  56.1 0.0 copy-start.10
  56.1 0.0 copy-start.9
  56.2 0.0 copy-start.8
  56.2 0.0 copy-start.7
  56.2 1.3 %copy.25 = f32[30,64,256]{2,1,0:T(8,128)} copy(f32[30,64,256]{2,1,0:T(8,128)S(1)} %get-tuple-element.30) | data formatting | bytes 3932160
  57.4 0.0 copy-done.6
  57.4 0.6 %copy.26 = f32[60,256]{1,0:T(8,128)} copy(f32[60,256]{1,0:T(8,128)S(1)} %copy-done.6) | data formatting | bytes 122880
  58.1 0.0 copy-done.5
  58.1 0.6 %copy.27 = f32[256,60]{0,1:T(8,128)} copy(f32[256,60]{0,1:T(8,128)S(1)} %bitcast.10) | data formatting | bytes 122880
  58.7 0.6 copy.28
  59.3 0.6 copy.29
  59.9 0.6 copy.30
  60.5 0.6 copy.31
  (7 shorter events, 0.0 us)
Async XLA Ops:
  0.6 1.5 %copy-start = (f32[30,64,256]{2,1,0:T(8,128)S(1)}, f32[30,64,256]{2,1,0:T(8,128)}, u32[]{:S(2)}) copy-start(f32[30,64,256]{2,1,0:T(8,128)} %seed_hbm.1) | copy-start | bytes 5898244
  2.2 1.2 %copy-start.1 = (bf16[30,64,256]{2,1,0:T(8,128)(2,1)S(1)}, bf16[30,64,256]{2,1,0:T(8,128)(2,1)}, u32[]{:S(2)}) copy-start(bf16[30,64,256]{2,1,0:T(8,128)(2,1)} %theta_hbm.1) | copy-start | bytes 2949124
  3.4 0.8 %copy-start.2 = (f32[60,256]{1,0:T(8,128)S(1)}, f32[60,256]{1,0:T(8,128)}, u32[]{:S(2)}) copy-start(f32[60,256]{1,0:T(8,128)} %w_in_ref.3) | copy-start | bytes 184324
  4.2 0.8 %copy-start.3 = (f32[256,60]{0,1:T(8,128)S(1)}, f32[256,60]{0,1:T(8,128)}, u32[]{:S(2)}) copy-start(f32[256,60]{0,1:T(8,128)} %param.17) | copy-start | bytes 184324
  41.3 0.7 %copy-start.4 = (f32[256,128]{1,0:T(8,128)}, f32[256,128]{1,0:T(8,128)S(1)}, u32[]{:S(2)}) copy-start(f32[256,128]{1,0:T(8,128)S(1)} %get-tuple-element.16) | copy-start | bytes 393220
  56.1 1.3 %copy-start.6 = (f32[60,256]{1,0:T(8,128)S(1)}, f32[60,256]{1,0:T(8,128)}, u32[]{:S(2)}) copy-start(f32[60,256]{1,0:T(8,128)} %get-tuple-element.31) | copy-start | bytes 184324
  56.1 2.0 %copy-start.5 = (f32[60,256]{1,0:T(8,128)S(1)}, f32[60,256]{1,0:T(8,128)}, u32[]{:S(2)}) copy-start(f32[60,256]{1,0:T(8,128)} %get-tuple-element.18) | copy-start | bytes 184324
  56.1 2.6 %copy-start.10 = (f32[16,60]{1,0:T(8,128)S(1)}, f32[16,60]{1,0:T(8,128)}, u32[]{:S(2)}) copy-start(f32[16,60]{1,0:T(8,128)} %get-tuple-element.19) | copy-start | bytes 11524
  56.1 3.2 %copy-start.9 = (f32[16,60]{1,0:T(8,128)S(1)}, f32[16,60]{1,0:T(8,128)}, u32[]{:S(2)}) copy-start(f32[16,60]{1,0:T(8,128)} %get-tuple-element.20) | copy-start | bytes 11524
  56.2 3.8 %copy-start.8 = (f32[16,60]{1,0:T(8,128)S(1)}, f32[16,60]{1,0:T(8,128)}, u32[]{:S(2)}) copy-start(f32[16,60]{1,0:T(8,128)} %get-tuple-element.35) | copy-start | bytes 11524
  56.2 4.4 %copy-start.7 = (f32[16,60]{1,0:T(8,128)S(1)}, f32[16,60]{1,0:T(8,128)}, u32[]{:S(2)}) copy-start(f32[16,60]{1,0:T(8,128)} %get-tuple-element.36) | copy-start | bytes 11524
